TPU v7x, 32 devices: a whole 2x2x4 slice. The times are simulated.
32 devices in a mesh: grp: 4 (over y, x), dev: 8 (over z, core).
Axes of the slice: x: 2, y: 2, z: 4, core: 2. Of those that a mesh axis runs over, the one named last changes fastest.
Arguments:
- memory: bfloat16 [65536, 512], P(('grp', 'dev')), may hold values from -6 to 6
- event_nodes: int32 [4096, 2], P(('grp', 'dev')), may hold values from 0 to 65535, as said below
- event_ticks: int32 [4096], P(('grp', 'dev')), may hold values from 0 to 99999
- neighbour_ids: int32 [4096, 20], P(('grp', 'dev')), may hold values from 0 to 65535, as said below
- neighbour_ticks: int32 [4096, 20], P(('grp', 'dev')), may hold values from 0 to 99999
- freq: float32 [128], replicated, may hold values from 1e-05 to 1
- phase: float32 [128], replicated, may hold values from -3.140625 to 3.140625
- w_msg1: bfloat16 [1152, 1024], replicated, may hold values from -0.1875 to 0.1875
- b_msg1: float32 [1024], replicated, may hold values from -3 to 3
- w_msg2: bfloat16 [1024, 512], replicated, may hold values from -0.1875 to 0.1875
- b_msg2: float32 [512], replicated, may hold values from -3 to 3
- w_query: bfloat16 [512, 512], replicated, may hold values from -1 to 1
- w_keyval: bfloat16 [640, 1024], replicated, may hold values from -1 to 1
- w_out: bfloat16 [512, 512], replicated, may hold values from -0.25 to 0.25
- gru_input: bfloat16 [512, 1536], replicated, may hold values from -0.25 to 0.25
- gru_hidden: bfloat16 [512, 1536], replicated, may hold values from -0.25 to 0.25
- gru_bias: float32 [2, 1536], replicated, may hold values from -3 to 3
Outputs:
- embedding: bfloat16 [4096, 512], P(('grp', 'dev'))
- new_memory: bfloat16 [65536, 512], P(('grp', 'dev'))
Inputs may be any that keep to these rules, and one draw needn't show every extreme that they name: `event_nodes`: node n is held by device n // 2048 of the grp-major order; of the 256 ids of one device's events, at most 16 belong to any one owner device. `neighbour_ids`: of the 2560 neighbour ids of one device's events, at most 160 belong to any one owner device.
All inputs are finite; a program needn't handle non-finite values.
Results may differ from a plain program's by a relative error of at most 0.01.
Values may be sent and summed in bfloat16 or wider, within the bound.
A program may use at most 128 MiB of HBM per device.

v0:
```python
import jax
import jax.numpy as jnp
from jax import lax
from jax.sharding import PartitionSpec as P

HDIM = 128


def encode(ticks, freq, phase):
    return jnp.cos(ticks.astype(jnp.float32)[..., None] * freq + phase).astype(jnp.bfloat16)


def take_rows(table, indices):
    flat = jnp.take(table, indices.reshape(-1), axis=0, mode="clip")
    return flat.reshape(indices.shape + (table.shape[1],))


def placing(node_ids, capacity, node_dev, owners):
    owner = node_ids // node_dev
    local_rows = node_ids % node_dev
    onehot = (owner[:, None] == jnp.arange(owners, dtype=jnp.int32)[None, :]).astype(jnp.int32)
    slot = jnp.sum(jnp.cumsum(onehot, axis=0) * onehot, axis=1) - 1
    position = owner * capacity + slot
    request = jnp.full((owners * capacity,), -1, jnp.int32).at[position].set(local_rows)
    return (position, request.reshape(owners, capacity))


def on_device(
    memory,
    event_nodes,
    event_ticks,
    neighbour_ids,
    neighbour_ticks,
    freq,
    phase,
    w_msg1,
    b_msg1,
    w_msg2,
    b_msg2,
    w_query,
    w_keyval,
    w_out,
    gru_input,
    gru_hidden,
    gru_bias,
):
    owners = lax.axis_size(("grp", "dev"))
    node_dev, width = memory.shape
    events = event_nodes.shape[0]
    fanout = neighbour_ids.shape[1]
    cap_e = 4 * events // owners
    cap_n = 2 * fanout * events // owners
    event_pos, event_req = placing(event_nodes.reshape(-1), cap_e, node_dev, owners)
    received = lax.all_to_all(event_req, ("grp", "dev"), split_axis=0, concat_axis=0, tiled=True)
    rows = take_rows(memory, received)
    event_rows = lax.all_to_all(rows, ("grp", "dev"), split_axis=0, concat_axis=0, tiled=True)
    pair = take_rows(event_rows.reshape(owners * cap_e, width), event_pos).reshape(events, 2, width)
    m_src = pair[:, 0]
    m_dst = pair[:, 1]
    enc = encode(event_ticks, freq, phase)
    inputs = jnp.concatenate(
        [
            jnp.concatenate([m_src, m_dst, enc], axis=1),
            jnp.concatenate([m_dst, m_src, enc], axis=1),
        ],
        axis=0,
    )
    hidden = jnp.maximum(
        jnp.dot(inputs, w_msg1, preferred_element_type=jnp.float32) + b_msg1, 0.0
    ).astype(jnp.bfloat16)
    messages = (jnp.dot(hidden, w_msg2, preferred_element_type=jnp.float32) + b_msg2).astype(
        jnp.bfloat16
    )
    paired_msgs = jnp.stack([messages[:events], messages[events:]], axis=1).reshape(
        2 * events, width
    )
    source_of_slot = (
        jnp.zeros((owners * cap_e,), jnp.int32)
        .at[event_pos]
        .set(jnp.arange(2 * events, dtype=jnp.int32))
    )
    outgoing = take_rows(paired_msgs, source_of_slot).reshape(owners, cap_e, width)
    arrived = lax.all_to_all(outgoing, ("grp", "dev"), split_axis=0, concat_axis=0, tiled=True)
    valid = (received >= 0).reshape(-1)
    target = jnp.maximum(received, 0).reshape(-1)
    terms = jnp.where(valid[:, None], arrived.reshape(-1, width).astype(jnp.float32), 0.0)
    sums = jnp.zeros((node_dev, width), jnp.float32).at[target].add(terms)
    counts = jnp.zeros((node_dev,), jnp.float32).at[target].add(valid.astype(jnp.float32))
    mean = (sums / jnp.maximum(counts, 1.0)[:, None]).astype(jnp.bfloat16)
    gate_in = jnp.dot(mean, gru_input, preferred_element_type=jnp.float32) + gru_bias[0]
    gate_hid = jnp.dot(memory, gru_hidden, preferred_element_type=jnp.float32) + gru_bias[1]
    reset = jax.nn.sigmoid(gate_in[:, :width] + gate_hid[:, :width])
    update = jax.nn.sigmoid(gate_in[:, width : 2 * width] + gate_hid[:, width : 2 * width])
    candidate = jnp.tanh(gate_in[:, 2 * width :] + reset * gate_hid[:, 2 * width :])
    fresh = (1.0 - update) * candidate + update * memory.astype(jnp.float32)
    new_memory = jnp.where(counts[:, None] > 0.0, fresh, memory.astype(jnp.float32)).astype(
        jnp.bfloat16
    )
    near_pos, near_req = placing(neighbour_ids.reshape(-1), cap_n, node_dev, owners)
    rows = take_rows(
        memory, lax.all_to_all(near_req, ("grp", "dev"), split_axis=0, concat_axis=0, tiled=True)
    )
    near_rows = lax.all_to_all(
        rows, ("grp", "dev"), split_axis=0, concat_axis=0, tiled=True
    ).reshape(owners * cap_n, width)
    m_near = take_rows(near_rows, near_pos).reshape(events, fanout, width)
    heads = width // HDIM
    query = (
        jnp.dot(m_src, w_query, preferred_element_type=jnp.float32)
        .astype(jnp.bfloat16)
        .reshape(events, heads, HDIM)
    )
    block = min(events, 128)
    blocks = events // block

    def embed_block(args):
        query_block, near_block, ticks_block, near_ticks = args
        dt_enc = encode(ticks_block[:, None] - near_ticks, freq, phase)
        feats = jnp.concatenate([near_block, dt_enc], axis=-1).reshape(block * fanout, -1)
        keyval = (
            jnp.dot(feats, w_keyval, preferred_element_type=jnp.float32)
            .astype(jnp.bfloat16)
            .reshape(block, fanout, 2, heads, HDIM)
        )
        scores = jnp.einsum(
            "ehc,ekhc->ehk", query_block, keyval[:, :, 0], preferred_element_type=jnp.float32
        ) / jnp.sqrt(jnp.float32(HDIM))
        scores = scores - jnp.max(scores, axis=-1, keepdims=True)
        expo = jnp.exp(scores)
        weights = (expo / jnp.sum(expo, axis=-1, keepdims=True)).astype(jnp.bfloat16)
        attn = (
            jnp.einsum(
                "ehk,ekhc->ehc", weights, keyval[:, :, 1], preferred_element_type=jnp.float32
            )
            .astype(jnp.bfloat16)
            .reshape(block, width)
        )
        return jnp.dot(attn, w_out, preferred_element_type=jnp.float32).astype(jnp.bfloat16)

    embedding = lax.map(
        embed_block,
        (
            query.reshape(blocks, block, heads, HDIM),
            m_near.reshape(blocks, block, fanout, width),
            event_ticks.reshape(blocks, block),
            neighbour_ticks.reshape(blocks, block, fanout),
        ),
    ).reshape(events, width)
    return (embedding, new_memory)


def solution(mesh):
    in_specs = (
        P(("grp", "dev"), None),
        P(("grp", "dev"), None),
        P(("grp", "dev")),
        P(("grp", "dev"), None),
        P(("grp", "dev"), None),
        P(),
        P(),
        P(),
        P(),
        P(),
        P(),
        P(),
        P(),
        P(),
        P(),
        P(),
        P(),
    )
    out_specs = (P(("grp", "dev"), None), P(("grp", "dev"), None))
    return jax.shard_map(
        on_device, mesh=mesh, in_specs=in_specs, out_specs=out_specs, check_vma=False
    )
```

profile of v0, /device:TPU:0, one launch (start us, length us, event | category | flops | bytes accessed | tf_op | source)
XLA Modules:
  0.0 253.4 jit_solution(13809934385158985435)
XLA Ops:
  0.6 0.9 copy.47
  1.6 0.1 reshape.408
  1.7 0.1 reshape.407
  1.9 0.1 reshape.406
  2.1 0.6 reduce-window.14
  2.6 0.2 slice_reduce_fusion
  2.9 0.1 fusion.59
  3.0 1.4 scatter_custom_fusion
  4.4 0.7 all_to_all.21
  5.1 7.3 %all-to-all-start = ((s32[32,1,16]{2,1,0:T(1,128)}), s32[32,1,16]{2,1,0:T(1,128)S(1)}, u32[]{:S(2)}, u32[]{:S(2)}) async-start(s32[32,1,16]{2,1,0:T(1,128)} %bitcast.3), calls=%async_computation | async-start | bytes 32768 | tf_op jit(solution)/shard_map/all_to_all | solution.py:54
  12.4 0.8 copy.53
  13.2 0.1 reshape.415
  13.4 9.2 %reduce-window.16 = s32[32,20,128]{2,1,0:T(8,128)S(1)} reduce-window(s32[32,20,128]{2,1,0:T(8,128)S(1)} %fusion.52, s32[]{:T(128)} %constant.95.clone.1), window={size=1x1x128 pad=0_0x0_0x127_0}, to_apply=%region_4.5 | reduce-window | flops 10403840 | bytes 655364 | tf_op jit(solution)/shard_map/reduce-window.2
  22.6 0.2 slice.86
  22.7 0.3 copy.67
  23.0 0.2 reduce-window.19
  23.2 0.2 broadcast_add_fusion
  23.4 0.1 reshape.414
  23.5 0.5 broadcast.503
  24.0 1.3 maximum_reduce_fusion
  25.4 4.5 %gather_fusion = bf16[512,512]{1,0:T(8,128)(2,1)} fusion(bf16[2048,512]{1,0:T(8,128)(2,1)} %param.17, s32[1024]{0:T(1024)S(1)} %pad_clamp_fusion.3), kind=kCustom, calls=%fused_computation | custom fusion | bytes 1050624 | tf_op jit(solution)/shard_map/jit(_take)/gather | solution.py:14
  29.9 5.8 %all-to-all-start.1 = ((bf16[32,16,512]{2,1,0:T(8,128)(2,1)}), bf16[32,16,512]{2,1,0:T(8,128)(2,1)S(1)}, u32[]{:S(2)}, u32[]{:S(2)}) async-start(bf16[32,16,512]{2,1,0:T(8,128)(2,1)} %bitcast.4), calls=%async_computation.1 | async-start | bytes 1048576 | tf_op jit(solution)/shard_map/all_to_all | solution.py:56
  35.8 0.1 reshape.413
  36.0 1.4 scatter_custom_fusion.3
  37.5 0.1 fusion.80
  37.6 9.9 %scatter_custom_fusion.1 = s32[5120]{0:T(1024)S(1)} fusion(s32[2560]{0:T(1024)S(1)} %get-tuple-element.27, s32[2560]{0:T(1024)S(1)} %get-tuple-element.46, s32[]{:T(128)} %constant.93.clone.1), kind=kCustom, calls=%fused_computation.123 | custom fusion | bytes 20484 | tf_op jit(solution)/shard_map/scatter | solution.py:24
  47.5 0.7 all_to_all.24
  48.3 0.3 cosine_convert_fusion.1
  48.6 3.6 %all-to-all-done.1 = bf16[32,16,512]{2,1,0:T(8,128)(2,1)S(1)} async-done(((bf16[32,16,512]{2,1,0:T(8,128)(2,1)}), bf16[32,16,512]{2,1,0:T(8,128)(2,1)S(1)}, u32[]{:S(2)}, u32[]{:S(2)}) %all-to-all-start.1) | async-done | bytes 524320 | tf_op jit(solution)/shard_map/all_to_all | solution.py:56
  52.1 2.6 %all-to-all-start.2 = ((s32[32,1,160]{2,1,0:T(1,128)}), s32[32,1,160]{2,1,0:T(1,128)S(1)}, u32[]{:S(2)}, u32[]{:S(2)}) async-start(s32[32,1,160]{2,1,0:T(1,128)} %all_to_all.24), calls=%async_computation.2 | async-start | bytes 65536 | tf_op jit(solution)/shard_map/all_to_all | solution.py:101
  54.7 1.2 gather_fusion.1
  55.9 0.1 reshape.412
  56.0 0.4 fusion.81
  56.4 2.4 fusion.25
  58.9 0.3 copy.60
  59.2 0.1 reshape.421
  59.3 2.6 %gather_fusion.4 = bf16[512,512]{1,0:T(8,128)(2,1)} fusion(bf16[256,512]{1,0:T(8,128)(2,1)S(1)} %reshape.421, s32[1024]{0:T(1024)S(1)} %pad_clamp_fusion.1), kind=kCustom, calls=%fused_computation.4 | custom fusion | bytes 1050624 | tf_op jit(solution)/shard_map/jit(_take)/gather | solution.py:14
  62.0 5.8 %all-to-all-start.4 = ((bf16[32,16,512]{2,1,0:T(8,128)(2,1)}), bf16[32,16,512]{2,1,0:T(8,128)(2,1)S(1)}, u32[]{:S(2)}, u32[]{:S(2)}) async-start(bf16[32,16,512]{2,1,0:T(8,128)(2,1)} %bitcast.22), calls=%async_computation.4 | async-start | bytes 1048576 | tf_op jit(solution)/shard_map/all_to_all | solution.py:83
  68.0 21.4 %gather_fusion.2 = bf16[5120,512]{1,0:T(8,128)(2,1)} fusion(bf16[2048,512]{1,0:T(8,128)(2,1)S(1)} %copy-done.2, s32[5120]{0:T(1024)S(1)} %broadcast_clamp_fusion), kind=kCustom, calls=%fused_computation.2 | custom fusion | bytes 10506240 | tf_op jit(solution)/shard_map/jit(_take)/gather | solution.py:14
  89.4 6.1 %all-to-all-start.3 = ((bf16[32,160,512]{2,1,0:T(8,128)(2,1)}), bf16[32,160,512]{2,1,0:T(8,128)(2,1)}, u32[]{:S(2)}, u32[]{:S(2)}) async-start(bf16[32,160,512]{2,1,0:T(8,128)(2,1)} %bitcast.88), calls=%async_computation.3 | async-start | bytes 10485760 | tf_op jit(solution)/shard_map/all_to_all | solution.py:103
  95.5 0.1 copy.58
  95.6 0.1 mul.91
  95.7 0.6 pad_clamp_fusion
  96.3 0.6 slice_reduce_fusion.2
  97.0 5.0 %cosine_convert_fusion = bf16[2560,128]{1,0:T(8,128)(2,1)S(1)} fusion(f32[128]{0:T(128)S(1)} %copy-done.16, f32[128]{0:T(128)S(1)} %copy-done.18, f32[2560]{0:T(1024)S(1)} %mul.91), kind=kLoop, calls=%fused_computation.46 | loop fusion | flops 983040 | bytes 666624 | tf_op jit(solution)/shard_map/while/body/eval_jaxpr/convert_element_type | solution.py:10
  102.0 7.8 %convolution_add_fusion = f32[2048,1536]{1,0:T(8,128)} fusion(bf16[2048,512]{1,0:T(8,128)(2,1)S(1)} %copy-done.2, bf16[512,1536]{1,0:T(8,128)(2,1)} %param.32, f32[1536]{0:T(1024)S(1)} %get-tuple-element.25), kind=kOutput, calls=%fused_computation.10 | convolution fusion | flops 3224371200 | bytes 16259072 | tf_op jit(solution)/shard_map/dot_general | solution.py:91
  109.9 0.1 ge.12
  110.1 3.6 %scatter_custom_fusion.2 = f32[2048]{0:T(1024)S(1)} fusion(s32[512]{0:T(512)S(1)} %reshape.482, f32[512]{0:T(512)S(1)} %convert_element_type.80, f32[]{:T(128)} %constant.105.clone.1), kind=kCustom, calls=%fused_computation.135 | custom fusion | flops 512 | bytes 8196 | tf_op jit(solution)/shard_map/scatter-add | solution.py:88
  113.7 0.6 broadcast_compare_fusion
  114.3 1.3 convolution_convert_fusion.2
  115.5 0.8 reshape.515
  116.3 6.1 %scatter_custom_fusion.4 = f32[2048,512]{1,0:T(8,128)} fusion(s32[512]{0:T(512)} %copy-done.14, f32[]{:T(128)} %constant.105.clone.1, bf16[512,512]{1,0:T(8,128)(2,1)S(1)} %bitcast.90, pred[512]{0:T(512)(128)(4,1)} %copy-done.13), kind=kCustom, calls=%fused_computation.42 | custom fusion | flops 786432 | bytes 4720128 | tf_op jit(solution)/shard_map/scatter-add | solution.py:87
  122.5 5.8 %convolution_add_fusion.1 = f32[2048,1536]{1,0:T(8,128)S(1)} fusion(bf16[512,1536]{1,0:T(8,128)(2,1)} %param.31, f32[1536]{0:T(1024)S(1)} %copy-done.11, f32[2048,512]{1,0:T(8,128)} %scatter_custom_fusion.4, f32[2048]{0:T(1024)S(1)} %broadcast_maximum_fusion), kind=kOutput, calls=%fused_computation.11 | convolution fusion | flops 3226468352 | bytes 18364416 | tf_op jit(solution)/shard_map/dot_general | solution.py:90
  128.3 8.6 %fusion.1 = bf16[2048,512]{1,0:T(8,128)(2,1)} fusion(bf16[2048,512]{1,0:T(8,128)(2,1)S(1)} %copy-done.2, f32[2048,1536]{1,0:T(8,128)} %convolution_add_fusion, f32[2048,1536]{1,0:T(8,128)S(1)} %convolution_add_fusion.1, pred[2048]{0:T(1024)(128)(4,1)S(1)} %copy-done.12), kind=kLoop, calls=%fused_computation.16 | loop fusion | flops 17825792 | bytes 29362176 | tf_op jit(solution)/shard_map/convert_element_type | solution.py:96
  136.9 75.9 %all-to-all-done.3 = bf16[32,160,512]{2,1,0:T(8,128)(2,1)} async-done(((bf16[32,160,512]{2,1,0:T(8,128)(2,1)}), bf16[32,160,512]{2,1,0:T(8,128)(2,1)}, u32[]{:S(2)}, u32[]{:S(2)}) %all-to-all-start.3) | async-done | bytes 5242912 | tf_op jit(solution)/shard_map/all_to_all | solution.py:103
  212.8 11.6 %gather_fusion.3 = bf16[2560,512]{1,0:T(8,128)(2,1)} fusion(bf16[5120,512]{1,0:T(8,128)(2,1)} %bitcast.12, s32[3072]{0:T(1024)S(1)} %copy-done.8), kind=kCustom, calls=%fused_computation.3 | custom fusion | bytes 5253120 | tf_op jit(solution)/shard_map/jit(_take)/gather | solution.py:14
  224.4 7.7 %convolution_convert_fusion = bf16[2560,1024]{1,0:T(8,128)(2,1)} fusion(bf16[640,1024]{1,0:T(8,128)(2,1)S(1)} %copy-done.20, bf16[2560,128]{1,0:T(8,128)(2,1)S(1)} %cosine_convert_fusion, bf16[2560,512]{1,0:T(8,128)(2,1)} %gather_fusion.3), kind=kOutput, calls=%fused_computation.12 | convolution fusion | flops 3364618240 | bytes 9830400 | tf_op jit(solution)/shard_map/while/body/eval_jaxpr/dot_general | solution.py:121
  232.2 9.3 %reshape.419 = bf16[128,20,2,4,128]{4,3,2,1,0:T(4,128)(2,1)} reshape(bf16[2560,1024]{1,0:T(8,128)(2,1)} %convolution_convert_fusion) | data formatting | bytes 10485760 | tf_op jit(solution)/shard_map/while/body/eval_jaxpr/reshape | solution.py:123
  241.5 5.9 %slice_bitcast_fusion = (bf16[128,20,4,128]{3,2,1,0:T(4,128)(2,1)}, bf16[128,20,4,128]{3,2,1,0:T(4,128)(2,1)S(1)}) fusion(bf16[128,20,2,4,128]{4,3,2,1,0:T(4,128)(2,1)} %reshape.419), kind=kLoop, calls=%fused_computation.39 | loop fusion | bytes 10485760 | tf_op jit(solution)/shard_map/while/body/eval_jaxpr/squeeze | solution.py:133
  247.4 1.7 fusion.18
  249.1 0.1 copy.63
  249.4 0.2 copy.64
  249.6 2.8 %fusion.16 = f32[128,4,1,128]{3,2,1,0:T(1,128)S(1)} fusion(bf16[128,4,20,1]{2,3,1,0:T(2,128)(2,1)S(1)} %copy.64, bf16[128,20,4,128]{3,2,1,0:T(4,128)(2,1)} %get-tuple-element.40), kind=kOutput, calls=%fused_computation.35 | convolution fusion | flops 2621440 | bytes 2904064 | tf_op jit(solution)/shard_map/while/body/eval_jaxpr/ehk,ekhc->ehc/dot_general | solution.py:132
  252.5 0.9 convolution_convert_fusion.1
  (82 shorter events, 1.1 us)
Async XLA Ops:
  0.6 55.8 %copy-start = (bf16[1152,1024]{1,0:T(8,128)(2,1)S(1)}, bf16[1152,1024]{1,0:T(8,128)(2,1)}, u32[]{:S(2)}) copy-start(bf16[1152,1024]{1,0:T(8,128)(2,1)} %param.24) | copy-start | bytes 7077892
  5.1 18.4 %all-to-all-start = ((s32[32,1,16]{2,1,0:T(1,128)}), s32[32,1,16]{2,1,0:T(1,128)S(1)}, u32[]{:S(2)}, u32[]{:S(2)}) async-start(s32[32,1,16]{2,1,0:T(1,128)} %bitcast.3), calls=%async_computation | async-start | bytes 32768 | tf_op jit(solution)/shard_map/all_to_all | solution.py:54
  23.2 12.7 %copy-start.19 = (s32[128]{0:T(128)S(1)}, s32[128]{0:T(128)}, u32[]{:S(2)}) copy-start(s32[128]{0:T(128)} %param.19) | copy-start | bytes 1540
  24.0 24.2 %copy-start.15 = (f32[128]{0:T(128)S(1)}, f32[128]{0:T(128)}, u32[]{:S(2)}) copy-start(f32[128]{0:T(128)} %param.23) | copy-start | bytes 1540
  24.0 24.2 %copy-start.17 = (f32[128]{0:T(128)S(1)}, f32[128]{0:T(128)}, u32[]{:S(2)}) copy-start(f32[128]{0:T(128)} %param.22) | copy-start | bytes 1540
  29.9 26.5 %copy-start.21 = (f32[1024]{0:T(1024)S(1)}, f32[1024]{0:T(1024)}, u32[]{:S(2)}) copy-start(f32[1024]{0:T(1024)} %param.25) | copy-start | bytes 12292
  29.9 26.5 %copy-start.22 = (f32[512]{0:T(512)S(1)}, f32[512]{0:T(512)}, u32[]{:S(2)}) copy-start(f32[512]{0:T(512)} %param.27) | copy-start | bytes 6148
  29.9 22.2 %all-to-all-start.1 = ((bf16[32,16,512]{2,1,0:T(8,128)(2,1)}), bf16[32,16,512]{2,1,0:T(8,128)(2,1)S(1)}, u32[]{:S(2)}, u32[]{:S(2)}) async-start(bf16[32,16,512]{2,1,0:T(8,128)(2,1)} %bitcast.4), calls=%async_computation.1 | async-start | bytes 1048576 | tf_op jit(solution)/shard_map/all_to_all | solution.py:56
  52.1 9.8 %all-to-all-start.2 = ((s32[32,1,160]{2,1,0:T(1,128)}), s32[32,1,160]{2,1,0:T(1,128)S(1)}, u32[]{:S(2)}, u32[]{:S(2)}) async-start(s32[32,1,160]{2,1,0:T(1,128)} %all_to_all.24), calls=%async_computation.2 | async-start | bytes 65536 | tf_op jit(solution)/shard_map/all_to_all | solution.py:101
  56.4 2.4 copy-start.4
  59.2 8.8 %copy-start.2 = (bf16[2048,512]{1,0:T(8,128)(2,1)S(1)}, bf16[2048,512]{1,0:T(8,128)(2,1)}, u32[]{:S(2)}) copy-start(bf16[2048,512]{1,0:T(8,128)(2,1)} %param.17) | copy-start | bytes 6291460
  62.0 27.4 %all-to-all-start.4 = ((bf16[32,16,512]{2,1,0:T(8,128)(2,1)}), bf16[32,16,512]{2,1,0:T(8,128)(2,1)S(1)}, u32[]{:S(2)}, u32[]{:S(2)}) async-start(bf16[32,16,512]{2,1,0:T(8,128)(2,1)} %bitcast.22), calls=%async_computation.4 | async-start | bytes 1048576 | tf_op jit(solution)/shard_map/all_to_all | solution.py:83
  89.3 6.2 %copy-start.10 = (s32[128,20]{0,1:T(8,128)S(1)}, s32[128,20]{0,1:T(8,128)}, u32[]{:S(2)}) copy-start(s32[128,20]{0,1:T(8,128)} %param.21) | copy-start | bytes 30724
  89.3 7.0 %copy-start.9 = (f32[2,1536]{1,0:T(2,128)S(1)}, f32[2,1536]{1,0:T(2,128)}, u32[]{:S(2)}) copy-start(f32[2,1536]{1,0:T(2,128)} %param.33) | copy-start | bytes 36868
  89.3 7.6 %copy-start.16 = (f32[128]{0:T(128)S(1)}, f32[128]{0:T(128)}, u32[]{:S(2)}) copy-start(f32[128]{0:T(128)} %param.23) | copy-start | bytes 1540
  89.4 7.6 %copy-start.18 = (f32[128]{0:T(128)S(1)}, f32[128]{0:T(128)}, u32[]{:S(2)}) copy-start(f32[128]{0:T(128)} %param.22) | copy-start | bytes 1540
  89.4 123.5 %all-to-all-start.3 = ((bf16[32,160,512]{2,1,0:T(8,128)(2,1)}), bf16[32,160,512]{2,1,0:T(8,128)(2,1)}, u32[]{:S(2)}, u32[]{:S(2)}) async-start(bf16[32,160,512]{2,1,0:T(8,128)(2,1)} %bitcast.88), calls=%async_computation.3 | async-start | bytes 10485760 | tf_op jit(solution)/shard_map/all_to_all | solution.py:103
  102.0 8.0 %copy-start.7 = (s32[32,16]{1,0:T(8,128)S(1)}, s32[32,16]{1,0:T(8,128)}, u32[]{:S(2)}) copy-start(s32[32,16]{1,0:T(8,128)} %get-tuple-element.22) | copy-start | bytes 6148
  102.0 12.3 %copy-start.5 = (bf16[128,512]{1,0:T(8,128)(2,1)S(1)}, bf16[128,512]{1,0:T(8,128)(2,1)}, u32[]{:S(2)}) copy-start(bf16[128,512]{1,0:T(8,128)(2,1)} %copy-done.4) | copy-start | bytes 393220
  109.9 12.6 %copy-start.11 = (f32[1536]{0:T(1024)S(1)}, f32[1536]{0:T(1024)}, u32[]{:S(2)}) copy-start(f32[1536]{0:T(1024)} %get-tuple-element.24) | copy-start | bytes 18436
  110.0 4.3 %copy-start.13 = (pred[512]{0:T(512)(128)(4,1)}, pred[512]{0:T(512)(128)(4,1)S(1)}, u32[]{:S(2)}) copy-start(pred[512]{0:T(512)(128)(4,1)S(1)} %ge.12) | copy-start | bytes 1540
  110.1 4.2 %copy-start.14 = (s32[512]{0:T(512)}, s32[512]{0:T(512)S(1)}, u32[]{:S(2)}) copy-start(s32[512]{0:T(512)S(1)} %reshape.482) | copy-start | bytes 6148
  122.5 5.8 %copy-start.12 = (pred[2048]{0:T(1024)(128)(4,1)S(1)}, pred[2048]{0:T(1024)(128)(4,1)}, u32[]{:S(2)}) copy-start(pred[2048]{0:T(1024)(128)(4,1)} %broadcast_compare_fusion) | copy-start | bytes 6148
  128.3 84.6 %copy-start.8 = (s32[3072]{0:T(1024)S(1)}, s32[3072]{0:T(1024)}, u32[]{:S(2)}) copy-start(s32[3072]{0:T(1024)} %pad_clamp_fusion) | copy-start | bytes 36868
  212.8 11.6 %copy-start.20 = (bf16[640,1024]{1,0:T(8,128)(2,1)S(1)}, bf16[640,1024]{1,0:T(8,128)(2,1)}, u32[]{:S(2)}) copy-start(bf16[640,1024]{1,0:T(8,128)(2,1)} %param.29) | copy-start | bytes 3932164
  241.5 5.9 %copy-start.6 = (bf16[128,4,128,1]{2,3,1,0:T(2,128)(2,1)S(1)}, bf16[128,4,128,1]{2,3,1,0:T(2,128)(2,1)}, u32[]{:S(2)}) copy-start(bf16[128,4,128,1]{2,3,1,0:T(2,128)(2,1)} %reshape.515) | copy-start | bytes 393220
  247.4 6.0 %copy-start.1 = (bf16[1152,1024]{1,0:T(8,128)(2,1)S(1)}, bf16[1152,1024]{1,0:T(8,128)(2,1)}, u32[]{:S(2)}) copy-start(bf16[1152,1024]{1,0:T(8,128)(2,1)} %param.24) | copy-start | bytes 7077892
  249.1 3.4 %copy-start.3 = (bf16[512,512]{1,0:T(8,128)(2,1)S(1)}, bf16[512,512]{1,0:T(8,128)(2,1)}, u32[]{:S(2)}) copy-start(bf16[512,512]{1,0:T(8,128)(2,1)} %param.30) | copy-start | bytes 1572868
where the time goes:
time: 254 us; the launch traced here: 253 us
  waiting for transfers between devices  79.5 us (31%)
  local copies, waits for them, and re-layouts  77.5 us (31%)
  other arithmetic  37.1 us (15%)
  matrix products  30.4 us (12%)
  starting transfers between devices  27.6 us (11%)
    all_to_all x2, waiting for transfers between devices, on_device(): lax.all_to_all(rows, ('grp', 'dev'), split_axis=0, concat_axis=0, tiled=T...  79.5 us
    gather x5, local copies, waits for them, and re-layouts, take_rows(): flat = jnp.take(table, indices.reshape(-1), axis=0, mode='clip')  41.2 us
    all_to_all x2, starting transfers between devices, on_device(): lax.all_to_all(rows, ('grp', 'dev'), split_axis=0, concat_axis=0, tiled=T...  12 us
    scatter x2, local copies, waits for them, and re-layouts, placing(): jnp.full((owners * capacity,), -1, jnp.int32).at[position].set(local_rows)  11.3 us
    another operation x5, other arithmetic  10.2 us
    reshape x1, local copies, waits for them, and re-layouts, embed_block(): keyval = jnp.dot(feats, w_keyval, preferred_element_type=jnp.float32).ast...  9.35 us
    convert_element_type x1, other arithmetic, on_device(): jnp.where(counts[:, None] > 0.0, fresh, memory.astype(jnp.float32))  8.64 us
    dot_general x1, matrix products, on_device(): jnp.dot(memory, gru_hidden, preferred_element_type=jnp.float32)  7.83 us
  transfers between devices with their start and end apart: 5, of which 2 were waited for; matrix products, arithmetic and copies ran while one was open for 37% of the time, Pallas kernels for 0%

commit v1 on v0

v1 whole, which is shorter than its diff:
```python
import functools

import jax
import jax.numpy as jnp
from jax import lax
from jax.experimental import pallas as pl
from jax.experimental.pallas import tpu as pltpu
from jax.sharding import PartitionSpec as P

HDIM = 128
LANE = 128
AXES = ("grp", "dev")
BF = jnp.bfloat16
F32 = jnp.float32


def encode(ticks, freq, phase):
    return jnp.cos(ticks.astype(F32)[..., None] * freq + phase).astype(BF)


def exchange(array):
    return lax.all_to_all(array, AXES, split_axis=0, concat_axis=0, tiled=True)


def contract_last(a, b):
    return lax.dot_general(a, b, (((1,), (1,)), ((), ())), preferred_element_type=F32)


def exclusive_sums(rows):
    m, n = rows.shape
    blocks = n // LANE
    flags = rows.astype(BF)
    upper = (jnp.arange(LANE)[:, None] < jnp.arange(LANE)[None, :]).astype(BF)
    inner = jnp.dot(flags.reshape(m * blocks, LANE), upper, preferred_element_type=F32)
    earlier = (jnp.arange(n)[:, None] < LANE * jnp.arange(blocks)[None, :]).astype(BF)
    before = jnp.dot(flags, earlier, preferred_element_type=F32)
    return (inner.reshape(m, blocks, LANE) + before[:, :, None]).reshape(m, n)


def slots_of(owner, owners):
    mine = owner[None, :] == jnp.arange(owners, dtype=jnp.int32)[:, None]
    return mine, jnp.sum(jnp.where(mine, exclusive_sums(mine), 0.0), axis=0).astype(jnp.int32)


def place(mine, slot, start, capacity, channels):
    owners, n = mine.shape
    left = jnp.concatenate([jnp.where(mine, c[None, :].astype(F32), 0.0).astype(BF) for c in channels])
    right = (slot[None, :] == start + jnp.arange(capacity, dtype=jnp.int32)[:, None]).astype(BF)
    out = contract_last(left, right).astype(jnp.int32)
    return [out[i * owners : (i + 1) * owners] for i in range(len(channels))]


def split_row(rows):
    return [rows // 256 + 1, rows % 256]


def join_row(parts):
    return (parts[0] - 1) * 256 + parts[1]


TICK_SHIFT = 131072


def split_info(event, delta):
    d = delta + TICK_SHIFT
    return [event + 1, d // 65536, (d // 256) % 256, d % 256]


def join_info(parts):
    event = parts[0] - 1
    delta = parts[1] * 65536 + parts[2] * 256 + parts[3] - TICK_SHIFT
    return event.reshape(-1), jnp.where(event < 0, 0, delta).reshape(-1)


def rows_at(table, rows):
    pick = (rows[:, None] == jnp.arange(table.shape[0], dtype=jnp.int32)[None, :]).astype(BF)
    return jnp.dot(pick, table, preferred_element_type=F32).astype(BF)


def attend_kernel(sizes, chunk, *refs):
    segments = len(sizes)
    xs, ds, es = refs[:segments], refs[segments : 2 * segments], refs[2 * segments : 3 * segments]
    qx_ref, qd_ref, wv_ref, wo_ref, out_ref, scores = refs[3 * segments :]
    rows = qx_ref.shape[0]
    events, width = out_ref.shape
    heads = rows // events
    scale = 1.0 / (HDIM**0.5)
    event = lax.broadcasted_iota(jnp.int32, (rows, 1), 0) % events
    top = jnp.full((rows, 1), -3.0e38, F32)
    steps = []
    base = 0
    for i, size in enumerate(sizes):
        for at in range(0, size, chunk):
            steps.append((i, at, min(chunk, size - at), base + at))
        base += size
    for i, at, length, column in steps:
        x = xs[i][at : at + length, :]
        d = ds[i][at : at + length, :]
        s = (contract_last(qx_ref[...], x) + contract_last(qd_ref[...], d)) * scale
        s = jnp.where(es[i][:, at : at + length] == event, s, -3.0e38)
        scores[:, column : column + length] = s
        top = jnp.maximum(top, jnp.max(s, axis=1, keepdims=True))
    total = jnp.zeros((rows, 1), F32)
    ctx_x = jnp.zeros((rows, width), F32)
    ctx_d = jnp.zeros((rows, qd_ref.shape[1]), F32)
    for i, at, length, column in steps:
        p = jnp.exp(scores[:, column : column + length] - top)
        total = total + jnp.sum(p, axis=1, keepdims=True)
        w = p.astype(BF)
        ctx_x = ctx_x + jnp.dot(w, xs[i][at : at + length, :], preferred_element_type=F32)
        ctx_d = ctx_d + jnp.dot(w, ds[i][at : at + length, :], preferred_element_type=F32)
    inverse = 1.0 / total
    ctx_x = (ctx_x * inverse).astype(BF)
    ctx_d = (ctx_d * inverse).astype(BF)
    parts = []
    for h in range(heads):
        r = slice(h * events, (h + 1) * events)
        c = slice(width + h * HDIM, width + (h + 1) * HDIM)
        part = jnp.dot(ctx_x[r], wv_ref[:width, c], preferred_element_type=F32)
        part = part + jnp.dot(ctx_d[r], wv_ref[width:, c], preferred_element_type=F32)
        parts.append(part.astype(BF))
    attn = jnp.concatenate(parts, axis=1)
    out_ref[...] = jnp.dot(attn, wo_ref[...], preferred_element_type=F32).astype(BF)


def attend(segments, qx, qd, w_keyval, w_out, events, width):
    sizes = tuple(x.shape[0] for x, _, _ in segments)
    rows, total = qx.shape[0], sum(sizes)
    features = width + qd.shape[1]
    args = (
        [x for x, _, _ in segments]
        + [d for _, d, _ in segments]
        + [e.reshape(1, -1) for _, _, e in segments]
        + [qx, qd, w_keyval, w_out]
    )
    return pl.pallas_call(
        functools.partial(attend_kernel, sizes, 512),
        out_shape=jax.ShapeDtypeStruct((events, width), BF),
        in_specs=[pl.BlockSpec(memory_space=pltpu.VMEM)] * len(args),
        out_specs=pl.BlockSpec(memory_space=pltpu.VMEM),
        scratch_shapes=[pltpu.VMEM((rows, total), F32)],
        compiler_params=pltpu.CompilerParams(vmem_limit_bytes=44 * 1024 * 1024),
        cost_estimate=pl.CostEstimate(
            flops=4 * rows * total * features,
            bytes_accessed=2 * total * features + 4 * 1024 * 1024,
            transcendentals=rows * total,
        ),
    )(*args)


def on_device(
    memory,
    event_nodes,
    event_ticks,
    neighbour_ids,
    neighbour_ticks,
    freq,
    phase,
    w_msg1,
    b_msg1,
    w_msg2,
    b_msg2,
    w_query,
    w_keyval,
    w_out,
    gru_input,
    gru_hidden,
    gru_bias,
):
    owners = lax.axis_size(AXES)
    me = lax.axis_index(AXES)
    node_dev, width = memory.shape
    events = event_nodes.shape[0]
    fanout = neighbour_ids.shape[1]
    cap_e = 4 * events // owners
    cap_n = 2 * fanout * events // owners
    base_n = 3 * cap_n // 5
    spill_n = fanout * events // owners
    spill_pad = -(-spill_n // LANE) * LANE

    ends = event_nodes.T.reshape(-1)
    end_mine, end_slot = slots_of(ends // node_dev, owners)
    end_req = join_row(place(end_mine, end_slot, 0, cap_e, split_row(ends % node_dev)))
    near = neighbour_ids.reshape(-1)
    near_mine, near_slot = slots_of(near // node_dev, owners)
    near_rows = split_row(near % node_dev)
    near_req = join_row(place(near_mine, near_slot, 0, base_n, near_rows))
    spilled = near_slot >= base_n
    spill_rank = exclusive_sums(spilled[None, :])[0].astype(jnp.int32)
    spill_mine = spilled[None, :]
    hi, mid, low = place(
        spill_mine, spill_rank, 0, spill_n, [near // 65536, (near // 256) % 256, near % 256]
    )
    (used,) = place(spill_mine, spill_rank, 0, spill_n, [jnp.ones_like(near)])
    spill_ids = jnp.where(used > 0, hi * 65536 + mid * 256 + low, -1)
    spill_count = jnp.sum(spilled.astype(jnp.int32)).reshape(1, 1)
    sent = jnp.concatenate(
        [
            end_req,
            near_req,
            jnp.broadcast_to(spill_ids, (owners, spill_n)),
            jnp.broadcast_to(spill_count, (owners, 1)),
        ],
        axis=1,
    )
    got = exchange(sent)
    end_got = got[:, :cap_e].reshape(-1)
    near_got = got[:, cap_e : cap_e + base_n].reshape(-1)
    spill_got = got[:, cap_e + base_n : cap_e + base_n + spill_n].reshape(-1)
    overfull = jnp.max(got[:, -1]) > spill_n

    states = rows_at(memory, end_got)
    end_rows = exchange(states.reshape(owners, cap_e, width)).reshape(-1, width)
    near_x = exchange(rows_at(memory, near_got).reshape(owners, base_n, width)).reshape(-1, width)
    spill_local = jnp.where(spill_got // node_dev == me, spill_got % node_dev, -1)
    spill_local = jnp.where(spill_got >= 0, spill_local, -1)
    spill_x = lax.psum_scatter(rows_at(memory, spill_local), AXES, scatter_dimension=0, tiled=True)
    spill_x = jnp.pad(spill_x, ((0, spill_pad - spill_n), (0, 0)))

    end_pos = (ends // node_dev) * cap_e + end_slot
    both = rows_at(end_rows, end_pos)
    m_src, m_dst = both[:events], both[events:]
    enc = encode(event_ticks, freq, phase)
    inputs = jnp.concatenate(
        [jnp.concatenate([m_src, m_dst, enc], axis=1), jnp.concatenate([m_dst, m_src, enc], axis=1)]
    )
    hidden = jnp.maximum(jnp.dot(inputs, w_msg1, preferred_element_type=F32) + b_msg1, 0.0).astype(BF)
    messages = (jnp.dot(hidden, w_msg2, preferred_element_type=F32) + b_msg2).astype(BF)
    slots = jnp.arange(owners * cap_e, dtype=jnp.int32)
    outgoing = jnp.dot(
        (slots[:, None] == end_pos[None, :]).astype(BF), messages, preferred_element_type=F32
    ).astype(BF)
    arrived = exchange(outgoing.reshape(owners, cap_e, width)).reshape(-1, width)

    valid = end_got >= 0
    same = jnp.logical_and(end_got[:, None] == end_got[None, :], valid[:, None])
    sums = jnp.dot(same.astype(BF), arrived, preferred_element_type=F32)
    counts = jnp.sum(same.astype(F32), axis=1)
    mean = (sums / jnp.maximum(counts, 1.0)[:, None]).astype(BF)
    gate_in = jnp.dot(mean, gru_input, preferred_element_type=F32) + gru_bias[0]
    gate_hid = jnp.dot(states, gru_hidden, preferred_element_type=F32) + gru_bias[1]
    reset = jax.nn.sigmoid(gate_in[:, :width] + gate_hid[:, :width])
    update = jax.nn.sigmoid(gate_in[:, width : 2 * width] + gate_hid[:, width : 2 * width])
    candidate = jnp.tanh(gate_in[:, 2 * width :] + reset * gate_hid[:, 2 * width :])
    fresh = ((1.0 - update) * candidate + update * states.astype(F32)).astype(BF)
    repeats = jnp.sum(jnp.logical_and(same, slots[None, :] < slots[:, None]).astype(F32), axis=1)
    first = jnp.where(jnp.logical_and(valid, repeats == 0.0), end_got, -1)
    chosen = jnp.arange(node_dev, dtype=jnp.int32)[:, None] == first[None, :]
    placed = jnp.dot(chosen.astype(BF), fresh, preferred_element_type=F32)
    touched = jnp.sum(chosen.astype(F32), axis=1) > 0.0
    new_memory = jnp.where(touched[:, None], placed.astype(BF), memory)

    heads = width // HDIM
    query = jnp.dot(m_src, w_query, preferred_element_type=F32).astype(BF)
    keys = w_keyval[:, :width].reshape(-1, heads, HDIM)
    lifted = jnp.einsum(
        "ehc,dhc->hed", query.reshape(events, heads, HDIM), keys, preferred_element_type=F32
    ).astype(BF)
    qx = lifted[:, :, :width].reshape(heads * events, width)
    qd = lifted[:, :, width:].reshape(heads * events, -1)
    near_event = jnp.repeat(jnp.arange(events, dtype=jnp.int32), fanout)
    delta = (event_ticks[:, None] - neighbour_ticks).reshape(-1)
    info = split_info(near_event, delta)

    def segment(x, parts, pad=0):
        event, ticks = join_info(parts)
        event = jnp.pad(event, (0, pad), constant_values=-1)
        ticks = jnp.pad(ticks, (0, pad))
        return (x, encode(ticks, freq, phase), event)

    base = segment(near_x, place(near_mine, near_slot, 0, base_n, info))

    spill = segment(spill_x, place(spill_mine, spill_rank, 0, spill_n, info), spill_pad - spill_n)

    def usual():
        return attend([base, spill], qx, qd, w_keyval, w_out, events, width)

    def crowded():
        rest_n = cap_n - base_n
        request = join_row(place(near_mine, near_slot, base_n, rest_n, near_rows))
        rows = rows_at(memory, exchange(request).reshape(-1))
        x = exchange(rows.reshape(owners, rest_n, width)).reshape(-1, width)
        rest = segment(x, place(near_mine, near_slot, base_n, rest_n, info))
        return attend([base, rest], qx, qd, w_keyval, w_out, events, width)

    embedding = lax.cond(overfull, crowded, usual)
    return (embedding, new_memory)


def solution(mesh):
    rows, flat = P(AXES, None), P(AXES)
    in_specs = (rows, rows, flat, rows, rows) + (P(),) * 12
    return jax.shard_map(
        on_device, mesh=mesh, in_specs=in_specs, out_specs=(rows, rows), check_vma=False
    )
```

time: 254 us -> 271 us (1.067)
  local copies, waits for them, and re-layouts: 77.5 us -> 12.3 us
  waiting for transfers between devices: 79.5 us -> 136 us
  other arithmetic: 37.1 us -> 17.9 us
  matrix products: 30.4 us -> 45.9 us
  between operations: 1.2 us -> 15.5 us
  loops' own time: 0 us -> 13.9 us
  Pallas kernels: 0 us -> 11.3 us
  starting transfers between devices: 27.6 us -> 16.5 us
    reduce_scatter x0 -> x1, waiting for transfers between devices: none -> 66.1 us  [on_device(): lax.psum_scatter(rows_at(memory, spill_local), AXES, scatter_dimension=0,...]
    gather x5 -> x0, local copies, waits for them, and re-layouts: 41.2 us -> none  [take_rows(): flat = jnp.take(table, indices.reshape(-1), axis=0, mode='clip')]
    dot_general x8 -> x23, matrix products: 30.4 us -> 45.9 us  [the longest x4 23.4 us: rows_at(): return jnp.dot(pick, table, preferred_element_type=F32).astype(BF)]
    another operation x0 -> x1, loops' own time: none -> 13.9 us  [on_device(): embedding = lax.cond(overfull, crowded, usual)]
    scatter x3 -> x0, local copies, waits for them, and re-layouts: 12.7 us -> none  [the longest x2 11.3 us: placing(): jnp.full((owners * capacity,), -1, jnp.int32).at[position].set(local_rows)]
    all_to_all x5 -> x4, starting transfers between devices: 27.6 us -> 16.2 us  [exchange(): return lax.all_to_all(array, AXES, split_axis=0, concat_axis=0, tiled=True)]
    pallas_call x0 -> x1, Pallas kernels: none -> 11.3 us  [attend(): pl.pallas_call(functools.partial(attend_kernel, sizes, 512), out_shape=ja...]
    another operation x6 -> x0, other arithmetic: 10.2 us -> none
  transfers between devices with their start and end apart: 5 -> 5, of which waited for: 2 -> 5; matrix products, arithmetic and copies ran while one was open for 37% -> 20% of each run, Pallas kernels for 0% -> 0%
where the time goes in v1:
time: 271 us; the launch traced here: 269 us
  waiting for transfers between devices  136 us (50%)
  matrix products  45.9 us (17%)
  other arithmetic  17.9 us (7%)
  starting transfers between devices  16.5 us (6%)
  between operations  15.5 us (6%)
  loops' own time  13.9 us (5%)
  local copies, waits for them, and re-layouts  12.3 us (5%)
  Pallas kernels  11.3 us (4%)
    all_to_all x4, waiting for transfers between devices, exchange(): return lax.all_to_all(array, AXES, split_axis=0, concat_axis=0, tiled=True)  70 us
    reduce_scatter x1, waiting for transfers between devices, on_device(): lax.psum_scatter(rows_at(memory, spill_local), AXES, scatter_dimension=0,...  66.1 us
    dot_general x4, matrix products, rows_at(): return jnp.dot(pick, table, preferred_element_type=F32).astype(BF)  23.4 us
    all_to_all x4, starting transfers between devices, exchange(): return lax.all_to_all(array, AXES, split_axis=0, concat_axis=0, tiled=True)  16.2 us
    another operation x1, loops' own time, on_device(): embedding = lax.cond(overfull, crowded, usual)  13.9 us
    pallas_call x1, Pallas kernels, attend(): pl.pallas_call(functools.partial(attend_kernel, sizes, 512), out_shape=ja...  11.3 us
    convert_element_type x5, other arithmetic, encode(): return jnp.cos(ticks.astype(F32)[..., None] * freq + phase).astype(BF)  7.58 us
    dot_general x1, matrix products, on_device(): placed = jnp.dot(chosen.astype(BF), fresh, preferred_element_type=F32)  6.87 us
  transfers between devices with their start and end apart: 5, of which 5 were waited for; matrix products, arithmetic and copies ran while one was open for 20% of the time, Pallas kernels for 0%

profile of v1, /device:TPU:0, one launch (start us, length us, event | category | flops | bytes accessed | tf_op | source)
XLA Modules:
  0.0 269.3 jit_solution(4627710010947881031)
XLA Ops:
  7.2 1.0 copy.49
  8.4 0.7 add_convert_fusion.2
  9.1 0.7 and_select_fusion.9
  9.8 0.6 negate_select_fusion.16
  10.4 0.2 fusion.113
  10.7 0.2 fusion.54
  10.9 0.6 convert_reduce_fusion.3
  11.6 0.7 subtract_add_fusion
  12.7 0.1 convert_element_type.543
  12.9 0.6 negate_select_fusion.5
  13.5 0.9 select_convert_fusion.9
  14.4 0.3 convolution_convert_fusion.7
  14.7 0.2 fusion.121
  14.9 0.2 fusion.57
  15.1 0.1 convolution_convert_fusion.8
  15.4 0.2 convolution_bitcast_fusion.1
  15.7 0.7 pad.37.clone
  16.5 0.4 fusion.174
  16.9 0.3 convolution_convert_fusion.10
  17.1 0.2 fusion.64
  17.5 0.7 copy.53
  18.2 7.3 %all-to-all-start.2 = ((s32[32,1,193]{2,1,0:T(1,128)}), s32[32,1,193]{2,1,0:T(1,128)S(1)}, u32[]{:S(2)}, u32[]{:S(2)}) async-start(s32[32,1,193]{2,1,0:T(1,128)} %copy.53), calls=%async_computation.2 | async-start | bytes 65536 | tf_op jit(solution)/shard_map/all_to_all | solution.py:22
  25.6 7.1 %all-to-all-done.2 = s32[32,1,193]{2,1,0:T(1,128)S(1)} async-done(((s32[32,1,193]{2,1,0:T(1,128)}), s32[32,1,193]{2,1,0:T(1,128)S(1)}, u32[]{:S(2)}, u32[]{:S(2)}) %all-to-all-start.2) | async-done | bytes 24736 | tf_op jit(solution)/shard_map/all_to_all | solution.py:22
  32.8 3.7 %fusion.51 = bf16[512,512]{1,0:T(8,128)(2,1)} fusion(bf16[2048,512]{1,0:T(8,128)(2,1)} %param.19, s32[512]{0:T(512)S(1)} %eq.298), kind=kOutput, calls=%fused_computation.90 | convolution fusion | flops 1075052544 | bytes 2623488 | tf_op jit(solution)/shard_map/dot_general | solution.py:77
  36.6 2.7 %all-to-all-start.4 = ((bf16[32,16,512]{2,1,0:T(8,128)(2,1)}), bf16[32,16,512]{2,1,0:T(8,128)(2,1)S(1)}, u32[]{:S(2)}, u32[]{:S(2)}) async-start(bf16[32,16,512]{2,1,0:T(8,128)(2,1)} %bitcast.23), calls=%async_computation.5 | async-start | bytes 1048576 | tf_op jit(solution)/shard_map/all_to_all | solution.py:22
  39.3 0.3 convolution_convert_fusion.9
  39.6 0.6 fusion.186
  40.2 0.9 cosine_convert_fusion.2
  41.4 14.2 %all-to-all-done.4 = bf16[32,16,512]{2,1,0:T(8,128)(2,1)S(1)} async-done(((bf16[32,16,512]{2,1,0:T(8,128)(2,1)}), bf16[32,16,512]{2,1,0:T(8,128)(2,1)S(1)}, u32[]{:S(2)}, u32[]{:S(2)}) %all-to-all-start.4) | async-done | bytes 524320 | tf_op jit(solution)/shard_map/all_to_all | solution.py:22
  55.7 0.3 convolution_convert_fusion.4
  56.1 0.9 fusion.49
  57.0 2.7 %convolution_convert_fusion.3 = bf16[512,512]{1,0:T(8,128)(2,1)} fusion(bf16[256,1024]{1,0:T(8,128)(2,1)S(1)} %fusion.49, bf16[1024,512]{1,0:T(8,128)(2,1)} %param.28, f32[512]{0:T(512)S(1)} %copy-done.35, s32[256]{0:T(256)S(1)} %multiply_add_fusion), kind=kOutput, calls=%fused_computation.88 | convolution fusion | flops 403308544 | bytes 2100224 | tf_op jit(solution)/shard_map/dot_general | solution.py:230
  59.7 2.6 all-to-all-start.5
  62.3 10.4 %fusion.41 = bf16[3072,512]{1,0:T(8,128)(2,1)} fusion(bf16[2048,512]{1,0:T(8,128)(2,1)} %param.19, s32[3072]{0:T(1024)S(1)} %eq.291), kind=kOutput, calls=%fused_computation.70 | convolution fusion | flops 6450315264 | bytes 5255168 | tf_op jit(solution)/shard_map/dot_general | solution.py:77
  72.7 6.0 %all-to-all-done.5 = bf16[32,16,512]{2,1,0:T(8,128)(2,1)S(1)} async-done(((bf16[32,16,512]{2,1,0:T(8,128)(2,1)}), bf16[32,16,512]{2,1,0:T(8,128)(2,1)S(1)}, u32[]{:S(2)}, u32[]{:S(2)}) %all-to-all-start.5) | async-done | bytes 524320 | tf_op jit(solution)/shard_map/all_to_all | solution.py:22
  78.7 0.8 copy-done.3
  79.5 3.5 %all-to-all-start.3 = ((bf16[32,96,512]{2,1,0:T(8,128)(2,1)}), bf16[32,96,512]{2,1,0:T(8,128)(2,1)}, u32[]{:S(2)}, u32[]{:S(2)}) async-start(bf16[32,96,512]{2,1,0:T(8,128)(2,1)} %bitcast.140), calls=%async_computation.4 | async-start | bytes 6291456 | tf_op jit(solution)/shard_map/all_to_all | solution.py:22
  83.0 0.3 reduce-scatter.2.cloned.1.call-start
  83.3 9.0 %fusion.40 = bf16[2560,512]{1,0:T(8,128)(2,1)} fusion(bf16[2048,512]{1,0:T(8,128)(2,1)} %param.19, s32[2560]{0:T(1024)S(1)} %fusion.156), kind=kOutput, calls=%fused_computation.69 | convolution fusion | flops 5375262720 | bytes 4728832 | tf_op jit(solution)/shard_map/dot_general | solution.py:77
  92.4 0.9 copy-done.8
  93.4 0.3 convolution_convert_fusion.6
  93.8 0.7 reshape.1023
  94.5 2.0 slice.134
  96.5 1.4 copy.64
  97.9 0.6 slice_reduce_fusion.2
  98.5 0.6 broadcast_compare_fusion.1
  99.1 0.7 iota_compare_fusion.35
  99.8 6.7 %cosine_convert_fusion.1 = bf16[3072,128]{1,0:T(8,128)(2,1)} fusion(f32[128]{0:T(128)S(1)} %copy-done.25, f32[128]{0:T(128)S(1)} %copy-done.26, f32[3072]{0:T(1024)S(1)} %convert_element_type.563), kind=kLoop, calls=%fused_computation.82 | loop fusion | flops 1179648 | bytes 799744 | tf_op jit(solution)/shard_map/convert_element_type | solution.py:18
  106.4 0.7 slice_reduce_fusion
  107.8 0.5 convert_reduce_fusion.1
  108.3 0.5 convert_reduce_fusion
  108.8 0.6 broadcast_maximum_fusion
  109.4 0.6 broadcast_compare_fusion.7
  110.0 4.3 %convolution_add_fusion = f32[512,1536]{1,0:T(8,128)} fusion(bf16[512,512]{1,0:T(8,128)(2,1)} %fusion.51, bf16[512,1536]{1,0:T(8,128)(2,1)} %param.34, f32[1536]{0:T(1024)S(1)} %get-tuple-element.181), kind=kOutput, calls=%fused_computation.76 | convolution fusion | flops 806092800 | bytes 5249024 | tf_op jit(solution)/shard_map/dot_general | solution.py:241
  114.3 0.2 fusion.55
  114.6 0.3 convolution_convert_fusion.2
  114.9 0.8 copy-done.1
  115.8 4.4 %convolution_add_fusion.1 = f32[512,1536]{1,0:T(8,128)} fusion(bf16[512,1536]{1,0:T(8,128)(2,1)} %param.33, f32[1536]{0:T(1024)} %get-tuple-element.180, bf16[512,512]{1,0:T(8,128)(2,1)S(1)} %bitcast.147, f32[512]{0:T(512)} %broadcast_maximum_fusion, s32[512]{0:T(512)S(1)} %eq.298, pred[512]{0:T(512)(128)(4,1)S(1)} %copy-done.31), kind=kOutput, calls=%fused_computation.77 | convolution fusion | flops 1075576832 | bytes 5253632 | tf_op jit(solution)/shard_map/dot_general | solution.py:240
  120.4 6.9 %fusion.45 = bf16[2048,512]{1,0:T(8,128)(2,1)} fusion(bf16[2048,512]{1,0:T(8,128)(2,1)} %param.19, s32[512]{0:T(512)S(1)} %copy-done.28, pred[2048]{0:T(1024)(128)(4,1)S(1)} %copy-done.29, f32[512,1536]{1,0:T(8,128)} %convolution_add_fusion, f32[512,1536]{1,0:T(8,128)} %convolution_add_fusion.1, bf16[512,512]{1,0:T(8,128)(2,1)} %fusion.51), kind=kOutput, calls=%fused_computation.79 | convolution fusion | flops 1081081856 | bytes 11014144 | tf_op jit(solution)/shard_map/dot_general | solution.py:249
  127.2 42.6 %all-to-all-done.3 = bf16[32,96,512]{2,1,0:T(8,128)(2,1)} async-done(((bf16[32,96,512]{2,1,0:T(8,128)(2,1)}), bf16[32,96,512]{2,1,0:T(8,128)(2,1)}, u32[]{:S(2)}, u32[]{:S(2)}) %all-to-all-start.3) | async-done | bytes 3145760 | tf_op jit(solution)/shard_map/all_to_all | solution.py:22
  169.9 66.1 %reduce-scatter.2.cloned.1.call-done = bf16[80,512]{1,0:T(8,128)(2,1)} async-done(((bf16[2560,512]{1,0:T(8,128)(2,1)}), bf16[80,512]{1,0:T(8,128)(2,1)}) %reduce-scatter.2.cloned.1.call-update) | async-done | bytes 81936 | tf_op jit(solution)/shard_map/reduce_scatter | solution.py:217
  236.2 26.0 %conditional.1 = (bf16[128,512]{1,0:T(8,128)(2,1)}) conditional(s32[]{:T(128)} %convert_element_type.540, (bf16[80,512]{1,0:T(8,128)(2,1)}, s32[3072]{0:T(1024)S(1)}, s32[1,80]{1,0:T(1,128)S(1)}, bf16[3072,512]{1,0:T(8,128)(2,1)}, bf16[3072,128]{1,0:T(8,128)(2,1)}, /*index=5*/bf16[128,128]{1,0:T(8,128)(2,1)S(1)}, bf16[512,512]{1,0:T(8,128)(2,1)S(1)}, ...), branch_computations={%region_5.6_spmd, %region_6.7_spmd} | conditional | flops 11079024640 | bytes 24311120 | solution.py:286
  250.0 0.9 pad.10.refs_1_
  250.9 11.3 %branch_0_fun.1 = bf16[128,512]{1,0:T(8,128)(2,1)} custom-call(bf16[3072,512]{1,0:T(8,128)(2,1)} %get-tuple-element.141.refs_0_, bf16[128,512]{1,0:T(8,128)(2,1)S(1)} %pad.10.refs_1_, bf16[3072,128]{1,0:T(8,128)(2,1)} %get-tuple-element.143.refs_2_, bf16[128,128]{1,0:T(8,128)(2,1)S(1)} %get-tuple-element.144.refs_3_, s32[1,3072]{1,0:T(1,128)S(1)} %bitcast.157, ...), custom_call_target="tpu_custom_call" | custom-call | flops 4194304000 | bytes 8290304 | tf_op jit(solution)/shard_map/cond/branch_0_fun/pallas_call | solution.py:136
  (119 shorter events, 2.2 us)
Async XLA Ops:
  7.2 48.9 %copy-start = (bf16[1152,1024]{1,0:T(8,128)(2,1)S(1)}, bf16[1152,1024]{1,0:T(8,128)(2,1)}, u32[]{:S(2)}) copy-start(bf16[1152,1024]{1,0:T(8,128)(2,1)} %param.26) | copy-start | bytes 7077892
  10.4 88.1 %copy-start.6 = (s32[2560]{0:T(1024)}, s32[2560]{0:T(1024)S(1)}, u32[]{:S(2)}) copy-start(s32[2560]{0:T(1024)S(1)} %get-tuple-element.185) | copy-start | bytes 30724
  10.9 81.4 %copy-start.22 = (s32[2560]{0:T(1024)}, s32[2560]{0:T(1024)S(1)}, u32[]{:S(2)}) copy-start(s32[2560]{0:T(1024)S(1)} %convert_bitcast_fusion) | copy-start | bytes 30724
  18.2 14.5 %all-to-all-start.2 = ((s32[32,1,193]{2,1,0:T(1,128)}), s32[32,1,193]{2,1,0:T(1,128)S(1)}, u32[]{:S(2)}, u32[]{:S(2)}) async-start(s32[32,1,193]{2,1,0:T(1,128)} %copy.53), calls=%async_computation.2 | async-start | bytes 65536 | tf_op jit(solution)/shard_map/all_to_all | solution.py:22
  32.8 6.8 %copy-start.32 = (s32[128]{0:T(128)S(1)}, s32[128]{0:T(128)}, u32[]{:S(2)}) copy-start(s32[128]{0:T(128)} %param.21) | copy-start | bytes 1540
  32.8 7.4 %copy-start.25 = (f32[128]{0:T(128)S(1)}, f32[128]{0:T(128)}, u32[]{:S(2)}) copy-start(f32[128]{0:T(128)} %param.25) | copy-start | bytes 1540
  32.8 7.4 %copy-start.26 = (f32[128]{0:T(128)S(1)}, f32[128]{0:T(128)}, u32[]{:S(2)}) copy-start(f32[128]{0:T(128)} %param.24) | copy-start | bytes 1540
  36.6 19.5 %copy-start.34 = (f32[1024]{0:T(1024)S(1)}, f32[1024]{0:T(1024)}, u32[]{:S(2)}) copy-start(f32[1024]{0:T(1024)} %param.27) | copy-start | bytes 12292
  36.6 19.1 %all-to-all-start.4 = ((bf16[32,16,512]{2,1,0:T(8,128)(2,1)}), bf16[32,16,512]{2,1,0:T(8,128)(2,1)S(1)}, u32[]{:S(2)}, u32[]{:S(2)}) async-start(bf16[32,16,512]{2,1,0:T(8,128)(2,1)} %bitcast.23), calls=%async_computation.5 | async-start | bytes 1048576 | tf_op jit(solution)/shard_map/all_to_all | solution.py:22
  56.1 0.9 copy-start.35
  59.7 19.0 %all-to-all-start.5 = ((bf16[32,16,512]{2,1,0:T(8,128)(2,1)}), bf16[32,16,512]{2,1,0:T(8,128)(2,1)S(1)}, u32[]{:S(2)}, u32[]{:S(2)}) async-start(bf16[32,16,512]{2,1,0:T(8,128)(2,1)} %bitcast.149), calls=%async_computation.6 | async-start | bytes 1048576 | tf_op jit(solution)/shard_map/all_to_all | solution.py:22
  78.7 0.8 copy-start.3
  79.5 90.4 %all-to-all-start.3 = ((bf16[32,96,512]{2,1,0:T(8,128)(2,1)}), bf16[32,96,512]{2,1,0:T(8,128)(2,1)}, u32[]{:S(2)}, u32[]{:S(2)}) async-start(bf16[32,96,512]{2,1,0:T(8,128)(2,1)} %bitcast.140), calls=%async_computation.4 | async-start | bytes 6291456 | tf_op jit(solution)/shard_map/all_to_all | solution.py:22
  83.0 153.0 %reduce-scatter.2.cloned.1.call-start = ((), (), s32[]{:S(2)}) async-start(), calls=%async_computation.7 | async-start | bytes 2703360 | tf_op jit(solution)/shard_map/reduce_scatter | solution.py:217
  92.3 0.9 copy-start.8
  92.3 1.0 copy-start.9
  92.3 1.1 copy-start.10
  93.7 4.1 %copy-start.19 = (f32[2,1536]{1,0:T(2,128)S(1)}, f32[2,1536]{1,0:T(2,128)}, u32[]{:S(2)}) copy-start(f32[2,1536]{1,0:T(2,128)} %param.35) | copy-start | bytes 36868
  107.8 0.5 copy-start.30
  108.3 6.0 %copy-start.27 = (s32[512]{0:T(512)}, s32[512]{0:T(512)S(1)}, u32[]{:S(2)}) copy-start(s32[512]{0:T(512)S(1)} %and_select_fusion.8) | copy-start | bytes 6148
  110.0 4.3 %copy-start.2 = (bf16[512,512]{1,0:T(8,128)(2,1)S(1)}, bf16[512,512]{1,0:T(8,128)(2,1)}, u32[]{:S(2)}) copy-start(bf16[512,512]{1,0:T(8,128)(2,1)} %param.30) | copy-start | bytes 1572868
  114.3 1.4 copy-start.31
  114.6 1.2 copy-start.4
  114.9 0.8 copy-start.1
  115.8 4.5 %copy-start.28 = (s32[512]{0:T(512)S(1)}, s32[512]{0:T(512)}, u32[]{:S(2)}) copy-start(s32[512]{0:T(512)} %copy-done.27) | copy-start | bytes 6148
  115.8 4.5 %copy-start.29 = (pred[2048]{0:T(1024)(128)(4,1)S(1)}, pred[2048]{0:T(1024)(128)(4,1)}, u32[]{:S(2)}) copy-start(pred[2048]{0:T(1024)(128)(4,1)} %broadcast_compare_fusion.7) | copy-start | bytes 6148
  120.2 115.8 %slice-start = ((bf16[4,128,640]{2,1,0:T(8,128)(2,1)}), bf16[4,128,512]{2,1,0:T(8,128)(2,1)S(1)}, s32[]{:S(2)}) async-start(bf16[4,128,640]{2,1,0:T(8,128)(2,1)} %copy-done.1), calls=%async_computation.8 | async-start | bytes 1048576 | tf_op jit(solution)/shard_map/slice | solution.py:259
  120.2 115.8 %slice-start.1 = ((bf16[4,128,640]{2,1,0:T(8,128)(2,1)}), bf16[4,128,128]{2,1,0:T(8,128)(2,1)S(1)}, s32[]{:S(2)}) async-start(bf16[4,128,640]{2,1,0:T(8,128)(2,1)} %copy-done.1), calls=%async_computation.9 | async-start | bytes 262144 | tf_op jit(solution)/shard_map/slice | solution.py:260
  120.2 115.8 %copy-start.5 = (pred[32,2560]{1,0:T(8,128)(4,1)S(1)}, pred[32,2560]{1,0:T(8,128)(4,1)}, u32[]{:S(2)}) copy-start(pred[32,2560]{1,0:T(8,128)(4,1)} %iota_compare_fusion.35) | copy-start | bytes 245764
  120.2 115.8 %copy-start.7 = (s32[2560]{0:T(1024)S(1)}, s32[2560]{0:T(1024)}, u32[]{:S(2)}) copy-start(s32[2560]{0:T(1024)} %copy-done.6) | copy-start | bytes 30724
  120.2 115.8 %copy-start.11 = (s32[2560]{0:T(1024)S(1)}, s32[2560]{0:T(1024)}, u32[]{:S(2)}) copy-start(s32[2560]{0:T(1024)} %get-tuple-element.184) | copy-start | bytes 30724
  120.3 115.8 %copy-start.12 = (s32[2560]{0:T(1024)S(1)}, s32[2560]{0:T(1024)}, u32[]{:S(2)}) copy-start(s32[2560]{0:T(1024)} %get-tuple-element.223) | copy-start | bytes 30724
  120.3 115.8 %copy-start.13 = (s32[2560]{0:T(1024)S(1)}, s32[2560]{0:T(1024)}, u32[]{:S(2)}) copy-start(s32[2560]{0:T(1024)} %get-tuple-element.225) | copy-start | bytes 30724
  120.3 115.8 %copy-start.14 = (s32[2560]{0:T(1024)S(1)}, s32[2560]{0:T(1024)}, u32[]{:S(2)}) copy-start(s32[2560]{0:T(1024)} %get-tuple-element.227) | copy-start | bytes 30724
  120.3 115.8 %copy-start.15 = (s32[2560]{0:T(1024)S(1)}, s32[2560]{0:T(1024)}, u32[]{:S(2)}) copy-start(s32[2560]{0:T(1024)} %get-tuple-element.228) | copy-start | bytes 30724
  120.3 115.8 %copy-start.16 = (s32[2560]{0:T(1024)S(1)}, s32[2560]{0:T(1024)}, u32[]{:S(2)}) copy-start(s32[2560]{0:T(1024)} %get-tuple-element.251) | copy-start | bytes 30724
  120.3 115.8 %copy-start.17 = (s32[2560]{0:T(1024)S(1)}, s32[2560]{0:T(1024)}, u32[]{:S(2)}) copy-start(s32[2560]{0:T(1024)} %get-tuple-element.253) | copy-start | bytes 30724
  120.3 115.8 %copy-start.18 = (bf16[128,128]{1,0:T(8,128)(2,1)S(1)}, bf16[128,128]{1,0:T(8,128)(2,1)}, u32[]{:S(2)}) copy-start(bf16[128,128]{1,0:T(8,128)(2,1)} %get-tuple-element.246) | copy-start | bytes 98308
  120.3 115.8 %copy-start.20 = (s32[3072]{0:T(1024)S(1)}, s32[3072]{0:T(1024)}, u32[]{:S(2)}) copy-start(s32[3072]{0:T(1024)} %reshape.1023) | copy-start | bytes 36868
  120.3 115.8 %copy-start.23 = (s32[2560]{0:T(1024)S(1)}, s32[2560]{0:T(1024)}, u32[]{:S(2)}) copy-start(s32[2560]{0:T(1024)} %copy-done.22) | copy-start | bytes 30724
  120.3 115.8 %copy-start.24 = (pred[2560]{0:T(1024)(128)(4,1)S(1)}, pred[2560]{0:T(1024)(128)(4,1)}, u32[]{:S(2)}) copy-start(pred[2560]{0:T(1024)(128)(4,1)} %get-tuple-element.255) | copy-start | bytes 7684
  120.4 115.8 %copy-start.33 = (s32[1,80]{1,0:T(1,128)S(1)}, s32[1,80]{1,0:T(1,128)}, u32[]{:S(2)}) copy-start(s32[1,80]{1,0:T(1,128)} %get-tuple-element.244) | copy-start | bytes 964
Sparse Core Ops, SparseCore 0:
  92.5 143.5 reduce-scatter.1

commit v2 on v1

--- a/solution.py
+++ b/solution.py
@@ -75,6 +75,23 @@
 def rows_at(table, rows):
     pick = (rows[:, None] == jnp.arange(table.shape[0], dtype=jnp.int32)[None, :]).astype(BF)
     return jnp.dot(pick, table, preferred_element_type=F32).astype(BF)
+
+
+def halving_sum(blocks, owners, me):
+    width = owners.bit_length() - 1
+    shape = blocks.shape[1:]
+    left = list(range(width - 1, -1, -1))
+    acc = blocks.reshape((2,) * width + shape)
+    for bit in [0] + list(range(3, width)) + [1, 2]:
+        axis = left.index(bit)
+        left.pop(axis)
+        low = lax.index_in_dim(acc, 0, axis, keepdims=False)
+        high = lax.index_in_dim(acc, 1, axis, keepdims=False)
+        upper = (me >> bit) % 2 == 1
+        pairs = [(i, i ^ (1 << bit)) for i in range(owners)]
+        came = lax.ppermute(jnp.where(upper, low, high), AXES, pairs)
+        acc = jnp.where(upper, high, low) + came
+    return acc
 
 
 def attend_kernel(sizes, chunk, *refs):
@@ -212,10 +229,6 @@
     states = rows_at(memory, end_got)
     end_rows = exchange(states.reshape(owners, cap_e, width)).reshape(-1, width)
     near_x = exchange(rows_at(memory, near_got).reshape(owners, base_n, width)).reshape(-1, width)
-    spill_local = jnp.where(spill_got // node_dev == me, spill_got % node_dev, -1)
-    spill_local = jnp.where(spill_got >= 0, spill_local, -1)
-    spill_x = lax.psum_scatter(rows_at(memory, spill_local), AXES, scatter_dimension=0, tiled=True)
-    spill_x = jnp.pad(spill_x, ((0, spill_pad - spill_n), (0, 0)))
 
     end_pos = (ends // node_dev) * cap_e + end_slot
     both = rows_at(end_rows, end_pos)
@@ -231,6 +244,12 @@
         (slots[:, None] == end_pos[None, :]).astype(BF), messages, preferred_element_type=F32
     ).astype(BF)
     arrived = exchange(outgoing.reshape(owners, cap_e, width)).reshape(-1, width)
+
+    spill_local = jnp.where(spill_got // node_dev == me, spill_got % node_dev, -1)
+    spill_local = jnp.where(spill_got >= 0, spill_local, -1)
+    spill_local, arrived = lax.optimization_barrier((spill_local, arrived))
+    spill_x = halving_sum(rows_at(memory, spill_local).reshape(owners, spill_n, width), owners, me)
+    spill_x = jnp.pad(spill_x, ((0, spill_pad - spill_n), (0, 0)))
 
     valid = end_got >= 0
     same = jnp.logical_and(end_got[:, None] == end_got[None, :], valid[:, None])

time: 271 us -> 186 us (0.69)
  waiting for transfers between devices: 136 us -> 36.6 us
  starting transfers between devices: 16.5 us -> 33.5 us
  between operations: 15.5 us -> 2.11 us
  local copies, waits for them, and re-layouts: 12.3 us -> 17.9 us
  other arithmetic: 17.9 us -> 22.3 us
    reduce_scatter x1 -> x0, waiting for transfers between devices: 66.1 us -> none  [on_device(): lax.psum_scatter(rows_at(memory, spill_local), AXES, scatter_dimension=0,...]
    all_to_all x4, waiting for transfers between devices: 70 us -> 9.56 us  [exchange(): return lax.all_to_all(array, AXES, split_axis=0, concat_axis=0, tiled=True)]
    ppermute x0 -> x5, waiting for transfers between devices: none -> 27.1 us  [halving_sum(): came = lax.ppermute(jnp.where(upper, low, high), AXES, pairs)]
    ppermute x0 -> x5, starting transfers between devices: none -> 13.2 us  [halving_sum(): came = lax.ppermute(jnp.where(upper, low, high), AXES, pairs)]
    all_to_all x4, starting transfers between devices: 16.2 us -> 20.3 us  [exchange(): return lax.all_to_all(array, AXES, split_axis=0, concat_axis=0, tiled=True)]
    unnamed x73 -> x55, local copies, waits for them, and re-layouts: 5.19 us -> 6.1 us
  transfers between devices with their start and end apart: 5 -> 9, of which waited for: 5 -> 7; matrix products, arithmetic and copies ran while one was open for 20% -> 34% of each run, Pallas kernels for 0% -> 0%
where the time goes in v2:
time: 186 us
  matrix products  48.1 us (26%)
  waiting for transfers between devices  36.6 us (20%)
  starting transfers between devices  33.5 us (18%)
  other arithmetic  22.3 us (12%)
  local copies, waits for them, and re-layouts  17.9 us (10%)
  loops' own time  13.9 us (7%)
  Pallas kernels  11.3 us (6%)
  between operations  2.11 us (1%)
    ppermute x5, waiting for transfers between devices, halving_sum(): came = lax.ppermute(jnp.where(upper, low, high), AXES, pairs)  27.1 us
    dot_general x4, matrix products, rows_at(): return jnp.dot(pick, table, preferred_element_type=F32).astype(BF)  23.4 us
    all_to_all x4, starting transfers between devices, exchange(): return lax.all_to_all(array, AXES, split_axis=0, concat_axis=0, tiled=True)  20.3 us
    another operation x1, loops' own time, on_device(): embedding = lax.cond(overfull, crowded, usual)  13.9 us
    ppermute x5, starting transfers between devices, halving_sum(): came = lax.ppermute(jnp.where(upper, low, high), AXES, pairs)  13.2 us
    pallas_call x1, Pallas kernels, attend(): pl.pallas_call(functools.partial(attend_kernel, sizes, 512), out_shape=ja...  11.3 us
    all_to_all x4, waiting for transfers between devices, exchange(): return lax.all_to_all(array, AXES, split_axis=0, concat_axis=0, tiled=True)  9.56 us
    convert_element_type x5, other arithmetic, encode(): return jnp.cos(ticks.astype(F32)[..., None] * freq + phase).astype(BF)  8.47 us
  transfers between devices with their start and end apart: 9, of which 7 were waited for; matrix products, arithmetic and copies ran while one was open for 34% of the time, Pallas kernels for 0%

profile of v2, /device:TPU:0, one launch (start us, length us, event | category | flops | bytes accessed | tf_op | source)
XLA Modules:
  0.0 185.7 jit_solution(11282788713854691686)
XLA Ops:
  0.7 1.0 copy.55
  1.9 0.7 add_convert_fusion.2
  2.6 0.7 and_select_fusion.9
  3.2 0.6 negate_select_fusion.16
  4.4 0.6 convert_reduce_fusion.3
  5.0 0.7 subtract_add_fusion
  6.3 0.6 negate_select_fusion.5
  8.4 0.7 pad.37.clone
  9.2 0.4 fusion.174
  10.3 0.7 copy.59
  10.9 7.3 %all-to-all-start.2 = ((s32[32,1,193]{2,1,0:T(1,128)}), s32[32,1,193]{2,1,0:T(1,128)S(1)}, u32[]{:S(2)}, u32[]{:S(2)}) async-start(s32[32,1,193]{2,1,0:T(1,128)} %copy.59), calls=%async_computation.2 | async-start | bytes 65536 | tf_op jit(solution)/shard_map/all_to_all | solution.py:22
  18.4 0.6 broadcast_compare_fusion.1
  19.0 0.7 iota_compare_fusion.35
  20.0 0.6 fusion.186
  21.0 1.1 cosine_convert_fusion.2
  22.1 0.6 multiply_add_fusion
  22.7 0.7 reshape.989
  23.4 2.0 %slice.175 = bf16[640,512]{1,0:T(8,128)(2,1)} slice(bf16[640,1024]{1,0:T(8,128)(2,1)} %param.31), slice={[0:640], [0:512]} | slice | bytes 1310720 | tf_op jit(solution)/shard_map/slice | solution.py:274
  25.4 1.4 copy.74
  26.8 0.6 copy-done.6
  27.5 3.7 %fusion.51 = bf16[512,512]{1,0:T(8,128)(2,1)} fusion(bf16[2048,512]{1,0:T(8,128)(2,1)} %param.19, s32[512]{0:T(512)S(1)} %eq.316), kind=kOutput, calls=%fused_computation.93 | convolution fusion | flops 1075052544 | bytes 2623488 | tf_op jit(solution)/shard_map/dot_general | solution.py:77
  31.2 5.8 %all-to-all-start.3 = ((bf16[32,16,512]{2,1,0:T(8,128)(2,1)}), bf16[32,16,512]{2,1,0:T(8,128)(2,1)S(1)}, u32[]{:S(2)}, u32[]{:S(2)}) async-start(bf16[32,16,512]{2,1,0:T(8,128)(2,1)} %bitcast.20), calls=%async_computation.3 | async-start | bytes 1048576 | tf_op jit(solution)/shard_map/all_to_all | solution.py:22
  37.1 1.4 slice_reduce_fusion.2
  38.5 7.3 %cosine_convert_fusion.1 = bf16[3072,128]{1,0:T(8,128)(2,1)} fusion(f32[128]{0:T(128)S(1)} %copy-done.21, f32[128]{0:T(128)} %param.24, f32[3072]{0:T(1024)S(1)} %convert_element_type.570), kind=kLoop, calls=%fused_computation.83 | loop fusion | flops 1179648 | bytes 799744 | tf_op jit(solution)/shard_map/convert_element_type | solution.py:18
  45.8 1.4 slice.197
  47.3 0.8 slice.212
  48.0 1.4 reshape.984
  49.4 0.7 eq.323
  50.1 0.7 fusion.156
  50.8 2.6 %all-to-all-done.3 = bf16[32,16,512]{2,1,0:T(8,128)(2,1)S(1)} async-done(((bf16[32,16,512]{2,1,0:T(8,128)(2,1)}), bf16[32,16,512]{2,1,0:T(8,128)(2,1)S(1)}, u32[]{:S(2)}, u32[]{:S(2)}) %all-to-all-start.3) | async-done | bytes 524320 | tf_op jit(solution)/shard_map/all_to_all | solution.py:22
  53.4 0.8 copy-done.4
  54.2 1.4 convolution_convert_fusion.4
  55.7 2.5 %fusion.49 = bf16[256,1024]{1,0:T(8,128)(2,1)} fusion(bf16[1152,1024]{1,0:T(8,128)(2,1)S(1)} %copy-done, bf16[128,128]{1,0:T(8,128)(2,1)} %get-tuple-element.266, bf16[128,512]{1,0:T(8,128)(2,1)S(1)} %get-tuple-element.232, bf16[128,512]{1,0:T(8,128)(2,1)S(1)} %get-tuple-element.231, f32[1024]{0:T(1024)} %param.27), kind=kOutput, calls=%fused_computation.90 | convolution fusion | flops 608305152 | bytes 3182592 | tf_op jit(solution)/shard_map/dot_general | solution.py:240
  58.2 2.9 %convolution_convert_fusion.3 = bf16[512,512]{1,0:T(8,128)(2,1)} fusion(bf16[256,1024]{1,0:T(8,128)(2,1)} %fusion.49, bf16[1024,512]{1,0:T(8,128)(2,1)} %param.28, f32[512]{0:T(512)S(1)} %copy-done.26, s32[256]{0:T(256)S(1)} %copy-done.23), kind=kOutput, calls=%fused_computation.91 | convolution fusion | flops 403308544 | bytes 2100224 | tf_op jit(solution)/shard_map/dot_general | solution.py:243
  61.1 3.6 %all-to-all-start.4 = ((bf16[32,16,512]{2,1,0:T(8,128)(2,1)}), bf16[32,16,512]{2,1,0:T(8,128)(2,1)}, u32[]{:S(2)}, u32[]{:S(2)}) async-start(bf16[32,16,512]{2,1,0:T(8,128)(2,1)} %bitcast.174), calls=%async_computation.4 | async-start | bytes 1048576 | tf_op jit(solution)/shard_map/all_to_all | solution.py:22
  64.8 10.4 %fusion.41 = bf16[3072,512]{1,0:T(8,128)(2,1)} fusion(bf16[2048,512]{1,0:T(8,128)(2,1)} %param.19, s32[3072]{0:T(1024)S(1)} %copy-done.14), kind=kOutput, calls=%fused_computation.71 | convolution fusion | flops 6450315264 | bytes 5255168 | tf_op jit(solution)/shard_map/dot_general | solution.py:77
  75.1 5.9 %all-to-all-done.4 = bf16[32,16,512]{2,1,0:T(8,128)(2,1)} async-done(((bf16[32,16,512]{2,1,0:T(8,128)(2,1)}), bf16[32,16,512]{2,1,0:T(8,128)(2,1)}, u32[]{:S(2)}, u32[]{:S(2)}) %all-to-all-start.4) | async-done | bytes 524320 | tf_op jit(solution)/shard_map/all_to_all | solution.py:22
  81.1 3.5 %all-to-all-start.5 = ((bf16[32,96,512]{2,1,0:T(8,128)(2,1)}), bf16[32,96,512]{2,1,0:T(8,128)(2,1)}, u32[]{:S(2)}, u32[]{:S(2)}) async-start(bf16[32,96,512]{2,1,0:T(8,128)(2,1)} %bitcast.165), calls=%async_computation.5 | async-start | bytes 6291456 | tf_op jit(solution)/shard_map/all_to_all | solution.py:22
  84.6 7.9 %fusion.40 = bf16[2560,512]{1,0:T(8,128)(2,1)S(1)} fusion(bf16[2048,512]{1,0:T(8,128)(2,1)} %param.19, s32[2560]{0:T(1024)S(1)} %fusion.156), kind=kOutput, calls=%fused_computation.70 | convolution fusion | flops 5375262720 | bytes 4728832 | tf_op jit(solution)/shard_map/dot_general | solution.py:77
  93.0 0.4 copy-done.11
  93.4 0.5 convert_reduce_fusion.1
  93.9 0.5 convert_reduce_fusion
  94.4 3.7 %convolution_add_fusion = f32[512,1536]{1,0:T(8,128)} fusion(bf16[512,512]{1,0:T(8,128)(2,1)} %fusion.51, bf16[512,1536]{1,0:T(8,128)(2,1)S(1)} %copy-done.25, f32[1536]{0:T(1024)S(1)} %copy-done.20), kind=kOutput, calls=%fused_computation.77 | convolution fusion | flops 806092800 | bytes 5249024 | tf_op jit(solution)/shard_map/dot_general | solution.py:260
  98.3 1.0 copy-done.1
  99.4 0.9 select_bitcast_fusion.1
  100.3 1.6 collective-permute-start.1
  101.9 0.7 slice_reduce_fusion
  103.2 0.6 broadcast_compare_fusion.7
  103.8 1.3 fusion.55
  105.5 0.8 copy-done.3
  106.3 20.4 %collective-permute-done.1 = bf16[2,2,2,80,512]{4,3,1,2,0:T(8,128)(2,1)} collective-permute-done((bf16[2,2,2,80,512]{4,3,1,2,0:T(8,128)(2,1)}, bf16[2,2,2,80,512]{4,3,1,2,0:T(8,128)(2,1)}, u32[]{:S(2)}, u32[]{:S(2)}) %collective-permute-start.1) | collective-permute-done | bytes 655392 | tf_op jit(solution)/shard_map/ppermute | solution.py:92
  126.7 1.2 bitcast_add_fusion.1
  127.9 1.7 collective-permute-start.2
  129.6 4.6 %convolution_add_fusion.1 = f32[512,1536]{1,0:T(8,128)} fusion(bf16[512,1536]{1,0:T(8,128)(2,1)} %param.33, f32[1536]{0:T(1024)S(1)} %copy-done.19, bf16[512,512]{1,0:T(8,128)(2,1)} %bitcast.23, f32[512]{0:T(512)S(1)} %broadcast_maximum_fusion, s32[512]{0:T(512)S(1)} %copy-done.11, pred[512]{0:T(512)(128)(4,1)S(1)} %broadcast_compare_fusion.8), kind=kOutput, calls=%fused_computation.78 | convolution fusion | flops 1075576832 | bytes 5253632 | tf_op jit(solution)/shard_map/dot_general | solution.py:259
  134.2 4.2 %collective-permute-done.2 = bf16[2,2,80,512]{3,2,0,1:T(8,128)(2,1)} collective-permute-done((bf16[2,2,80,512]{3,2,0,1:T(8,128)(2,1)S(1)}, bf16[2,2,80,512]{3,2,0,1:T(8,128)(2,1)}, u32[]{:S(2)}, u32[]{:S(2)}) %collective-permute-start.2) | collective-permute-done | bytes 327712 | tf_op jit(solution)/shard_map/ppermute | solution.py:92
  138.4 1.0 bitcast_add_fusion.2
  139.5 4.3 %collective-permute-start.3 = (bf16[2,80,512]{2,1,0:T(8,128)(2,1)S(1)}, bf16[2,80,512]{2,1,0:T(8,128)(2,1)S(1)}, u32[]{:S(2)}, u32[]{:S(2)}) collective-permute-start(bf16[2,80,512]{2,1,0:T(8,128)(2,1)S(1)} %select_bitcast_fusion.3), channel_id=1, source_target_pairs={{0,2},{1,3},{2,0},{3,1},{4,6},{5,7},{6,4},{7,5},{8,10},{9,11},{10,... | collective-permute-start | bytes 491528 | tf_op jit(solution)/shard_map/ppermute | solution.py:92
  143.9 6.6 %fusion.45 = bf16[2048,512]{1,0:T(8,128)(2,1)} fusion(bf16[2048,512]{1,0:T(8,128)(2,1)} %param.19, s32[512]{0:T(512)S(1)} %and_select_fusion.8, pred[2048]{0:T(1024)(128)(4,1)} %broadcast_compare_fusion.7, f32[512,1536]{1,0:T(8,128)} %convolution_add_fusion, f32[512,1536]{1,0:T(8,128)} %convolution_add_fusion.1, bf16[512,512]{1,0:T(8,128)(2,1)} %fusion.51), kind=kOutput, calls=%fused_computation.80 | convolution fusion | flops 1081081856 | bytes 11014144 | tf_op jit(solution)/shard_map/dot_general | solution.py:268
  150.7 5.5 %collective-permute-start.4 = (bf16[80,512]{1,0:T(8,128)(2,1)S(1)}, bf16[80,512]{1,0:T(8,128)(2,1)S(1)}, u32[]{:S(2)}, u32[]{:S(2)}) collective-permute-start(bf16[80,512]{1,0:T(8,128)(2,1)S(1)} %broadcast_select_fusion), channel_id=1, source_target_pairs={{0,4},{1,5},{2,6},{3,7},{4,0},{5,1},{6,2},{7,3},{8,12},{9,13},{10,... | collective-permute-start | bytes 245768 | tf_op jit(solution)/shard_map/ppermute | solution.py:92
  156.2 1.0 all-to-all-done.5
  157.3 2.3 %collective-permute-done.4 = bf16[80,512]{1,0:T(8,128)(2,1)S(1)} collective-permute-done((bf16[80,512]{1,0:T(8,128)(2,1)S(1)}, bf16[80,512]{1,0:T(8,128)(2,1)S(1)}, u32[]{:S(2)}, u32[]{:S(2)}) %collective-permute-start.4) | collective-permute-done | bytes 81952 | tf_op jit(solution)/shard_map/ppermute | solution.py:92
  159.7 25.8 %conditional.1 = (bf16[128,512]{1,0:T(8,128)(2,1)}) conditional(s32[]{:T(128)} %convert_element_type.540, (pred[]{:T(512)}, bf16[80,512]{1,0:T(8,128)(2,1)S(1)}, bf16[80,512]{1,0:T(8,128)(2,1)S(1)}, bf16[80,512]{1,0:T(8,128)(2,1)S(1)}, s32[3072]{0:T(1024)}, /*index=5*/s32[1,80]{1,0:T(1,128)}, bf16[3072,512]{1,0:T(8,128)(2,1)}, ...), branch_computations={%region_4.5_spmd, %region_5.6_spmd} | conditional | flops 11079024640 | bytes 24302928 | solution.py:305
  173.5 0.7 pad_bitcast_fusion.refs_5_
  174.2 11.3 %branch_0_fun.1 = bf16[128,512]{1,0:T(8,128)(2,1)} custom-call(bf16[3072,512]{1,0:T(8,128)(2,1)} %get-tuple-element.150.refs_0_, bf16[128,512]{1,0:T(8,128)(2,1)S(1)} %pad.10.refs_1_, bf16[3072,128]{1,0:T(8,128)(2,1)} %get-tuple-element.155.refs_2_, bf16[128,128]{1,0:T(8,128)(2,1)} %get-tuple-element.156.refs_3_, s32[1,3072]{1,0:T(1,128)} %bitcast.182, ...), custom_call_target="tpu_custom_call" | custom-call | flops 4194304000 | bytes 8290304 | tf_op jit(solution)/shard_map/cond/branch_0_fun/pallas_call | solution.py:153
  (120 shorter events, 5.7 us)
Async XLA Ops:
  0.6 55.0 %copy-start = (bf16[1152,1024]{1,0:T(8,128)(2,1)S(1)}, bf16[1152,1024]{1,0:T(8,128)(2,1)}, u32[]{:S(2)}) copy-start(bf16[1152,1024]{1,0:T(8,128)(2,1)} %param.26) | copy-start | bytes 7077892
  3.9 14.5 %copy-start.8 = (s32[2560]{0:T(1024)}, s32[2560]{0:T(1024)S(1)}, u32[]{:S(2)}) copy-start(s32[2560]{0:T(1024)S(1)} %get-tuple-element.201) | copy-start | bytes 30724
  4.4 14.0 %copy-start.24 = (s32[128]{0:T(128)S(1)}, s32[128]{0:T(128)}, u32[]{:S(2)}) copy-start(s32[128]{0:T(128)} %param.21) | copy-start | bytes 1540
  4.4 16.2 %copy-start.15 = (s32[2560]{0:T(1024)}, s32[2560]{0:T(1024)S(1)}, u32[]{:S(2)}) copy-start(s32[2560]{0:T(1024)S(1)} %convert_bitcast_fusion) | copy-start | bytes 30724
  6.3 0.8 copy-start.12
  9.6 11.4 %copy-start.21 = (f32[128]{0:T(128)S(1)}, f32[128]{0:T(128)}, u32[]{:S(2)}) copy-start(f32[128]{0:T(128)} %param.25) | copy-start | bytes 1540
  9.6 11.4 %copy-start.22 = (f32[128]{0:T(128)S(1)}, f32[128]{0:T(128)}, u32[]{:S(2)}) copy-start(f32[128]{0:T(128)} %param.24) | copy-start | bytes 1540
  10.9 15.8 %all-to-all-start.2 = ((s32[32,1,193]{2,1,0:T(1,128)}), s32[32,1,193]{2,1,0:T(1,128)S(1)}, u32[]{:S(2)}, u32[]{:S(2)}) async-start(s32[32,1,193]{2,1,0:T(1,128)} %copy.59), calls=%async_computation.2 | async-start | bytes 65536 | tf_op jit(solution)/shard_map/all_to_all | solution.py:22
  26.8 0.6 copy-start.6
  27.5 3.7 %copy-start.10 = (s32[512]{0:T(512)}, s32[512]{0:T(512)S(1)}, u32[]{:S(2)}) copy-start(s32[512]{0:T(512)S(1)} %eq.316) | copy-start | bytes 6148
  31.2 22.2 %all-to-all-start.3 = ((bf16[32,16,512]{2,1,0:T(8,128)(2,1)}), bf16[32,16,512]{2,1,0:T(8,128)(2,1)S(1)}, u32[]{:S(2)}, u32[]{:S(2)}) async-start(bf16[32,16,512]{2,1,0:T(8,128)(2,1)} %bitcast.20), calls=%async_computation.3 | async-start | bytes 1048576 | tf_op jit(solution)/shard_map/all_to_all | solution.py:22
  53.4 0.8 copy-start.4
  55.7 2.5 %copy-start.23 = (s32[256]{0:T(256)S(1)}, s32[256]{0:T(256)}, u32[]{:S(2)}) copy-start(s32[256]{0:T(256)} %multiply_add_fusion) | copy-start | bytes 3076
  55.7 2.5 %copy-start.26 = (f32[512]{0:T(512)S(1)}, f32[512]{0:T(512)}, u32[]{:S(2)}) copy-start(f32[512]{0:T(512)} %param.29) | copy-start | bytes 6148
  58.2 6.6 %copy-start.14 = (s32[3072]{0:T(1024)S(1)}, s32[3072]{0:T(1024)}, u32[]{:S(2)}) copy-start(s32[3072]{0:T(1024)} %eq.323) | copy-start | bytes 36868
  61.1 19.9 %all-to-all-start.4 = ((bf16[32,16,512]{2,1,0:T(8,128)(2,1)}), bf16[32,16,512]{2,1,0:T(8,128)(2,1)}, u32[]{:S(2)}, u32[]{:S(2)}) async-start(bf16[32,16,512]{2,1,0:T(8,128)(2,1)} %bitcast.174), calls=%async_computation.4 | async-start | bytes 1048576 | tf_op jit(solution)/shard_map/all_to_all | solution.py:22
  81.1 76.2 %all-to-all-start.5 = ((bf16[32,96,512]{2,1,0:T(8,128)(2,1)}), bf16[32,96,512]{2,1,0:T(8,128)(2,1)}, u32[]{:S(2)}, u32[]{:S(2)}) async-start(bf16[32,96,512]{2,1,0:T(8,128)(2,1)} %bitcast.165), calls=%async_computation.5 | async-start | bytes 6291456 | tf_op jit(solution)/shard_map/all_to_all | solution.py:22
  92.7 0.7 copy-start.11
  92.7 1.7 copy-start.20
  92.7 1.7 copy-start.25
  92.9 5.3 %collective-permute-start = (bf16[2,2,2,2,80,512]{5,4,2,3,0,1:T(8,128)(2,1)S(1)}, bf16[2,2,2,2,80,512]{5,4,2,3,0,1:T(8,128)(2,1)S(1)}, u32[]{:S(2)}, u32[]{:S(2)}) collective-permute-start(bf16[2,2,2,2,80,512]{5,4,2,3,0,1:T(8,128)(2,1)S(1)} %select_bitcast_fusion), channel_id=1, source_target_pairs={{0,1},{1,0},{2,3},{3,2},{4,5},{5,4},{6,7},{7,6},{8,9},{9,8},{10,11... | collective-permute-start | bytes 3932168 | tf_op jit(solution)/shard_map/ppermute | solution.py:92
  98.1 3.7 %copy-start.7 = (s32[32,1,193]{2,0,1:T(8,128)S(1)}, s32[32,1,193]{2,0,1:T(8,128)}, u32[]{:S(2)}) copy-start(s32[32,1,193]{2,0,1:T(8,128)} %copy-done.6) | copy-start | bytes 74116
  98.3 1.1 copy-start.1
  100.3 26.3 %collective-permute-start.1 = (bf16[2,2,2,80,512]{4,3,1,2,0:T(8,128)(2,1)}, bf16[2,2,2,80,512]{4,3,1,2,0:T(8,128)(2,1)}, u32[]{:S(2)}, u32[]{:S(2)}) collective-permute-start(bf16[2,2,2,80,512]{4,3,1,2,0:T(8,128)(2,1)} %select_bitcast_fusion.1), channel_id=1, source_target_pairs={{0,8},{1,9},{2,10},{3,11},{4,12},{5,13},{6,14},{7,15},{8,0},{9,1},... | collective-permute-start | bytes 1966088 | tf_op jit(solution)/shard_map/ppermute | solution.py:92
  103.2 23.4 %copy-start.2 = (bf16[2,2,2,2,80,512]{5,4,2,3,0,1:T(8,128)(2,1)S(1)}, bf16[2,2,2,2,80,512]{5,4,2,3,0,1:T(8,128)(2,1)}, u32[]{:S(2)}) copy-start(bf16[2,2,2,2,80,512]{5,4,2,3,0,1:T(8,128)(2,1)} %copy-done.1) | copy-start | bytes 3932164
  105.4 0.8 copy-start.3
  105.5 24.1 %copy-start.19 = (f32[1536]{0:T(1024)S(1)}, f32[1536]{0:T(1024)}, u32[]{:S(2)}) copy-start(f32[1536]{0:T(1024)} %get-tuple-element.196) | copy-start | bytes 18436
  127.9 10.5 %collective-permute-start.2 = (bf16[2,2,80,512]{3,2,0,1:T(8,128)(2,1)S(1)}, bf16[2,2,80,512]{3,2,0,1:T(8,128)(2,1)}, u32[]{:S(2)}, u32[]{:S(2)}) collective-permute-start(bf16[2,2,80,512]{3,2,0,1:T(8,128)(2,1)S(1)} %select_bitcast_fusion.2), channel_id=1, source_target_pairs={{0,16},{1,17},{2,18},{3,19},{4,20},{5,21},{6,22},{7,23},{8,24},{9,... | collective-permute-start | bytes 983048 | tf_op jit(solution)/shard_map/ppermute | solution.py:92
  139.5 20.1 %slice-start = ((bf16[4,128,640]{2,1,0:T(8,128)(2,1)}), bf16[4,128,512]{2,1,0:T(8,128)(2,1)S(1)}, s32[]{:S(2)}) async-start(bf16[4,128,640]{2,1,0:T(8,128)(2,1)} %copy-done.3), calls=%async_computation.6 | async-start | bytes 1048576 | tf_op jit(solution)/shard_map/slice | solution.py:278
  139.5 20.1 %slice-start.1 = ((bf16[4,128,640]{2,1,0:T(8,128)(2,1)}), bf16[4,128,128]{2,1,0:T(8,128)(2,1)S(1)}, s32[]{:S(2)}) async-start(bf16[4,128,640]{2,1,0:T(8,128)(2,1)} %copy-done.3), calls=%async_computation.7 | async-start | bytes 262144 | tf_op jit(solution)/shard_map/slice | solution.py:279
  139.5 20.1 %copy-start.5 = (pred[32,2560]{1,0:T(8,128)(4,1)S(1)}, pred[32,2560]{1,0:T(8,128)(4,1)}, u32[]{:S(2)}) copy-start(pred[32,2560]{1,0:T(8,128)(4,1)} %iota_compare_fusion.35) | copy-start | bytes 245764
  139.5 20.1 %copy-start.9 = (s32[2560]{0:T(1024)S(1)}, s32[2560]{0:T(1024)}, u32[]{:S(2)}) copy-start(s32[2560]{0:T(1024)} %copy-done.8) | copy-start | bytes 30724
  139.5 20.1 %copy-start.13 = (pred[2560]{0:T(1024)(128)(4,1)S(1)}, pred[2560]{0:T(1024)(128)(4,1)}, u32[]{:S(2)}) copy-start(pred[2560]{0:T(1024)(128)(4,1)} %copy-done.12) | copy-start | bytes 7684
  139.5 20.1 %copy-start.17 = (pred[2560]{0:T(1024)(128)(4,1)S(1)}, pred[2560]{0:T(1024)(128)(4,1)}, u32[]{:S(2)}) copy-start(pred[2560]{0:T(1024)(128)(4,1)} %get-tuple-element.274) | copy-start | bytes 7684
  139.5 20.1 %copy-start.18 = (pred[2560]{0:T(1024)(128)(4,1)S(1)}, pred[2560]{0:T(1024)(128)(4,1)}, u32[]{:S(2)}) copy-start(pred[2560]{0:T(1024)(128)(4,1)} %get-tuple-element.275) | copy-start | bytes 7684
  139.5 11.1 %collective-permute-start.3 = (bf16[2,80,512]{2,1,0:T(8,128)(2,1)S(1)}, bf16[2,80,512]{2,1,0:T(8,128)(2,1)S(1)}, u32[]{:S(2)}, u32[]{:S(2)}) collective-permute-start(bf16[2,80,512]{2,1,0:T(8,128)(2,1)S(1)} %select_bitcast_fusion.3), channel_id=1, source_target_pairs={{0,2},{1,3},{2,0},{3,1},{4,6},{5,7},{6,4},{7,5},{8,10},{9,11},{10,... | collective-permute-start | bytes 491528 | tf_op jit(solution)/shard_map/ppermute | solution.py:92
  150.7 8.9 %collective-permute-start.4 = (bf16[80,512]{1,0:T(8,128)(2,1)S(1)}, bf16[80,512]{1,0:T(8,128)(2,1)S(1)}, u32[]{:S(2)}, u32[]{:S(2)}) collective-permute-start(bf16[80,512]{1,0:T(8,128)(2,1)S(1)} %broadcast_select_fusion), channel_id=1, source_target_pairs={{0,4},{1,5},{2,6},{3,7},{4,0},{5,1},{6,2},{7,3},{8,12},{9,13},{10,... | collective-permute-start | bytes 245768 | tf_op jit(solution)/shard_map/ppermute | solution.py:92
